TPU v7x, 32 devices: a whole 2x2x4 slice. The times are simulated.
32 devices in a mesh: walk: 16 (over z, x, core), elec: 2 (over y).
Axes of the slice: x: 2, y: 2, z: 4, core: 2. Of those that a mesh axis runs over, the one named last changes fastest.
Arguments:
- positions: float32 [96, 3, 200], P('walk', None, 'elec'), may hold values from -5 to 5
- targets: bfloat16 [96, 200, 3200], P('walk', 'elec'), may hold values from -6 to 6
- w_in: float32 [4, 256], replicated, may hold values from -3 to 3
- v_in: float32 [4, 32], replicated, may hold values from -3 to 3
- w_up: float32 [2, 256, 32], replicated, may hold values from -0.375 to 0.375
- w_gate: float32 [2, 32, 32], replicated, may hold values from -1 to 1
- w_mix: float32 [2, 256, 256], replicated, may hold values from -0.375 to 0.375
- w_msg: float32 [2, 32, 256], replicated, may hold values from -1 to 1
- bias: float32 [2, 256], replicated, may hold values from -3 to 3
- w_head: bfloat16 [256, 3200], replicated, may hold values from -0.375 to 0.375
Outputs:
- grad_head: float32 [3200, 256], P('walk')
- grad_in: float32 [4, 256], replicated
- grad_up: float32 [2, 256, 32], replicated
- grad_gate: float32 [2, 32, 32], replicated
- grad_mix: float32 [2, 256, 256], replicated
- grad_msg: float32 [2, 32, 256], replicated
- grad_bias: float32 [2, 256], replicated
All inputs are finite; a program needn't handle non-finite values.
Results may differ from a plain program's by a relative error of at most 0.0003.
Values sent between devices are 32-bit elements; how exact they have to be, the bound alone decides.
A program may use at most 192 MiB of HBM per device.

v0:
```python
import jax
import jax.numpy as jnp
from jax import lax
from jax.sharding import PartitionSpec as P

LAYERS = 2


HI = lax.Precision.HIGHEST


def embed_states(pos_rows, w_in):
    radius = jnp.sqrt(jnp.sum(pos_rows * pos_rows, axis=1) + 1.0)
    feats = jnp.concatenate([pos_rows, radius[:, None, :]], axis=1)
    return jnp.tanh(jnp.einsum("wci,ch->wih", feats, w_in, precision=HI))


def embed_pairs(pos_rows, pos_all, v_in):
    diff = pos_rows[:, :, :, None] - pos_all[:, :, None, :]
    dist = jnp.sqrt(jnp.sum(diff * diff, axis=1) + 1.0)
    feats = jnp.concatenate([diff, dist[:, None]], axis=1)
    return jnp.tanh(jnp.einsum("wcie,cp->wiep", feats, v_in, precision=HI))


def layer_update(h_rows, s_all, pairs, w_mix, w_msg, bias, w_gate):
    gates = jax.nn.sigmoid(jnp.einsum("wiep,pq->wieq", pairs, w_gate, precision=HI))
    message = jnp.einsum("wieq,weq->wiq", gates, s_all, precision=HI) / s_all.shape[1]
    pre = jnp.einsum("wih,hk->wik", h_rows, w_mix, precision=HI)
    pre = pre + jnp.einsum("wiq,qk->wik", message, w_msg, precision=HI) + bias
    return jnp.tanh(pre) + h_rows


def on_device(positions, targets, w_in, v_in, w_up, w_gate, w_mix, w_msg, bias, w_head):
    walkers = positions.shape[0] * lax.axis_size("walk")
    pos_all = lax.all_gather(positions, "elec", axis=2, tiled=True)
    pairs = embed_pairs(positions, pos_all, v_in)
    states, pull_in = jax.vjp(lambda weight: embed_states(positions, weight), w_in)
    saved_states = []
    saved_proj = []
    for layer in range(LAYERS):
        up_now = w_up[layer]
        local_proj = jnp.einsum("wjh,hp->wjp", states, up_now, precision=HI)
        proj = lax.all_gather(local_proj, "elec", axis=1, tiled=True)
        saved_states.append(states)
        saved_proj.append(proj)
        states = layer_update(
            states, proj, pairs, w_mix[layer], w_msg[layer], bias[layer], w_gate[layer]
        )
    last = states.reshape(-1, states.shape[2]).astype(jnp.bfloat16)
    orbitals = jnp.dot(last, w_head, preferred_element_type=jnp.float32)
    flat_targets = targets.reshape(-1, targets.shape[2]).astype(jnp.float32)
    d_orb = (2.0 / walkers * (orbitals - flat_targets)).astype(jnp.bfloat16)
    head_part = lax.psum_scatter(
        lax.dot_general(d_orb, last, (((0,), (0,)), ((), ())), preferred_element_type=jnp.float32),
        "walk",
        scatter_dimension=0,
        tiled=True,
    )
    d_states = lax.dot_general(
        d_orb, w_head, (((1,), (1,)), ((), ())), preferred_element_type=jnp.float32
    )
    d_states = d_states.reshape(states.shape)
    grads_up = [None] * LAYERS
    grads_gate = [None] * LAYERS
    grads_mix = [None] * LAYERS
    grads_msg = [None] * LAYERS
    grads_bias = [None] * LAYERS
    for layer in reversed(range(LAYERS)):

        def local_layer(h_rows, s_all, mix, msg, shift, gate):
            return layer_update(h_rows, s_all, pairs, mix, msg, shift, gate)

        _, pull = jax.vjp(
            local_layer,
            saved_states[layer],
            saved_proj[layer],
            w_mix[layer],
            w_msg[layer],
            bias[layer],
            w_gate[layer],
        )
        d_rows, d_proj, d_mix, d_msg, d_bias, d_gate = pull(d_states)
        d_proj_own = lax.psum_scatter(d_proj, "elec", scatter_dimension=1, tiled=True)
        grads_up[layer] = jnp.einsum("wjh,wjp->hp", saved_states[layer], d_proj_own, precision=HI)
        d_states = d_rows + jnp.einsum("wjp,hp->wjh", d_proj_own, w_up[layer], precision=HI)
        grads_gate[layer] = d_gate
        grads_mix[layer] = d_mix
        grads_msg[layer] = d_msg
        grads_bias[layer] = d_bias
    grad_in = pull_in(d_states)[0]
    grad_up = jnp.stack(grads_up)
    grad_gate = jnp.stack(grads_gate)
    grad_mix = jnp.stack(grads_mix)
    grad_msg = jnp.stack(grads_msg)
    grad_bias = jnp.stack(grads_bias)
    grad_in, grad_up, grad_gate, grad_mix, grad_msg, grad_bias = lax.psum(
        (grad_in, grad_up, grad_gate, grad_mix, grad_msg, grad_bias), ("walk", "elec")
    )
    grad_head = lax.psum(head_part, "elec")
    return (grad_head, grad_in, grad_up, grad_gate, grad_mix, grad_msg, grad_bias)


def solution(mesh):
    return jax.shard_map(
        on_device,
        mesh=mesh,
        in_specs=(
            P("walk", None, "elec"),
            P("walk", "elec", None),
            P(),
            P(),
            P(),
            P(),
            P(),
            P(),
            P(),
            P(),
        ),
        out_specs=(P("walk", None), P(), P(), P(), P(), P(), P()),
        check_vma=False,
    )
```

profile of v0, /device:TPU:0, one launch (start us, length us, event | category | flops | bytes accessed | tf_op | source)
XLA Modules:
  0.0 474.8 jit_solution(301974054413448681)
XLA Ops:
  15.3 13.1 %all_gather.13 = f32[6,200,32]{2,0,1:T(8,128)S(1)} all-gather(f32[6,100,32]{2,0,1:T(8,128)S(1)} %copy.41), channel_id=1, replica_groups=mesh['walk'=16,'elec'=2] {'elec'}, dimensions={1}, use_global_device_ids=true | all-gather | bytes 230400 | tf_op jit(solution)/shard_map/all_gather | solution.py:43
  29.3 7.1 %all_gather.14 = f32[6,3,200]{0,1,2:T(4,128)S(1)} all-gather(f32[6,3,100]{0,1,2:T(4,128)} %copy.43), channel_id=1, replica_groups=mesh['walk'=16,'elec'=2] {'elec'}, dimensions={2}, use_global_device_ids=true | all-gather | bytes 21600 | tf_op jit(solution)/shard_map/all_gather | solution.py:35
  36.7 3.9 broadcast_subtract_fusion
  43.3 19.8 %fusion.30 = f32[6,100,200,32]{2,3,1,0:T(8,128)} fusion(f32[6,1,100,200]{3,1,2,0:T(1,128)S(1)} %copy.46, f32[6,3,100,200]{3,1,2,0:T(4,128)} %get-tuple-element.19, f32[4,32]{1,0:T(4,128)} %param.13), kind=kOutput, calls=%fused_computation.31 | convolution fusion | flops 184800000 | bytes 17280512 | tf_op jit(solution)/shard_map/wcie,cp->wiep/dot_general | solution.py:22
  63.1 28.5 %multiply_reduce_fusion.1 = (f32[6,32,100]{1,2,0:T(8,128)S(1)}, f32[6,100,200,32]{2,3,1,0:T(8,128)}) fusion(f32[6,32,200]{2,1,0:T(8,128)S(1)} %copy-done.11, f32[2,32,32]{2,1,0:T(8,128)S(1)} %copy-done.18, f32[6,100,200,32]{2,3,1,0:T(8,128)} %fusion.30), kind=kOutput, calls=%fused_computation.13 | convolution fusion | flops 1493740800 | bytes 31009792 | tf_op jit(solution)/shard_map/wiep,pq->wieq/dot_general | solution.py:26
  96.5 14.7 %all_gather.15 = f32[6,200,32]{2,0,1:T(8,128)} all-gather(f32[6,100,32]{2,0,1:T(8,128)} %copy.48), channel_id=1, replica_groups=mesh['walk'=16,'elec'=2] {'elec'}, dimensions={1}, use_global_device_ids=true | all-gather | bytes 230400 | tf_op jit(solution)/shard_map/all_gather | solution.py:43
  111.2 2.1 copy.88
  113.2 28.6 %multiply_reduce_fusion = (f32[6,32,100]{1,2,0:T(8,128)}, f32[6,100,200,32]{2,3,1,0:T(8,128)}) fusion(f32[6,32,200]{2,1,0:T(8,128)} %copy.88, f32[2,32,32]{2,1,0:T(8,128)} %param.15, f32[6,100,200,32]{2,3,1,0:T(8,128)} %fusion.30), kind=kOutput, calls=%fused_computation.12 | convolution fusion | flops 1493740800 | bytes 35310592 | tf_op jit(solution)/shard_map/wiep,pq->wieq/dot_general | solution.py:26
  147.1 5.9 %reshape.61 = f32[600,3200]{1,0:T(8,128)} reshape(bf16[6,100,3200]{2,1,0:T(8,128)(2,1)} %param.11) | data formatting | bytes 11520000 | tf_op jit(solution)/shard_map/convert_element_type | solution.py:51
  153.0 4.4 multiply_convert_fusion
  159.2 2.1 fusion.117
  161.3 2.0 reshape.60
  163.3 1.9 fusion.113
  167.4 26.3 %fusion.2 = f32[6,32,1,200]{3,2,1,0:T(1,128)S(1)} fusion(f32[6,32,100,1]{2,3,1,0:T(1,128)S(1)} %bitcast.196, f32[6,100,200,32]{2,3,1,0:T(8,128)} %get-tuple-element.28), kind=kOutput, calls=%fused_computation.4 | convolution fusion | flops 46080000 | bytes 15590400 | tf_op jit(solution)/shard_map/transpose(jvp(wieq,weq->wiq))/dot_general | solution.py:27
  194.7 5.3 %fusion.116 = f32[3200,256]{1,0:T(8,128)} fusion(bf16[600,3200]{1,0:T(8,128)(2,1)} %copy-done.1, bf16[600,256]{1,0:T(8,128)(2,1)} %copy-done.3), kind=kOutput, calls=%fused_computation.141 | convolution fusion | flops 983040000 | bytes 7424000 | tf_op jit(solution)/shard_map/dot_general | solution.py:54
  200.1 2.0 convolution_bitcast_fusion
  203.8 24.5 %fusion.39 = f32[1,32,32]{2,1,0:T(8,128)} fusion(f32[6,100,200,32]{2,3,1,0:T(8,128)} %get-tuple-element.28, f32[6,32,200]{2,1,0:T(8,128)} %copy.88, f32[6,32,100]{1,2,0:T(8,128)} %copy.52, f32[6,100,200,32]{2,3,1,0:T(8,128)} %fusion.30), kind=kOutput, calls=%fused_computation.57 | convolution fusion | flops 1489920000 | bytes 30954496 | tf_op jit(solution)/shard_map/transpose(jvp(wiep,pq->wieq))/dot_general | solution.py:26
  231.4 2.7 convolution_add_fusion.1
  234.1 3.7 fusion.112
  240.0 26.7 %fusion = f32[6,32,1,200]{3,2,1,0:T(1,128)S(1)} fusion(f32[6,32,100,1]{2,3,1,0:T(1,128)S(1)} %bitcast.198, f32[6,100,200,32]{2,3,1,0:T(8,128)} %get-tuple-element.24), kind=kOutput, calls=%fused_computation.2 | convolution fusion | flops 46080000 | bytes 15590400 | tf_op jit(solution)/shard_map/transpose(jvp(wieq,weq->wiq))/dot_general | solution.py:27
  269.1 24.1 %fusion.44 = f32[1,32,32]{2,1,0:T(8,128)S(1)} fusion(f32[6,100,200,32]{2,3,1,0:T(8,128)} %get-tuple-element.24, f32[6,32,200]{2,1,0:T(8,128)} %copy.87, f32[6,32,100]{1,2,0:T(8,128)} %copy.50, f32[6,100,200,32]{2,3,1,0:T(8,128)} %fusion.30), kind=kOutput, calls=%fused_computation.58 | convolution fusion | flops 1489920000 | bytes 30954496 | tf_op jit(solution)/shard_map/transpose(jvp(wiep,pq->wieq))/dot_general | solution.py:26
  301.5 23.3 %all-reduce.13.cloned.1.call-done = (f32[200,256]{1,0:T(8,128)}, f32[6,200,32]{1,2,0:T(8,128)}) async-done(((f32[200,256]{1,0:T(8,128)}, f32[6,200,32]{1,2,0:T(8,128)}), (f32[200,256]{1,0:T(8,128)}, f32[6,200,32]{1,2,0:T(8,128)})) %all-reduce.13.cloned.1.call-update) | async-done | bytes 358416 | tf_op jit(solution)/shard_map/psum | solution.py:99
  330.6 40.5 %all-reduce.2 = (f32[4,256]{1,0:T(4,128)}, f32[2,32,32]{2,1,0:T(8,128)}, f32[2,256]{1,0:T(2,128)}) all-reduce(f32[4,256]{1,0:T(4,128)S(1)} %convolution_bitcast_fusion.6, f32[2,32,32]{2,1,0:T(8,128)} %pad_maximum_fusion.3, f32[2,256]{1,0:T(2,128)} %pad_maximum_fusion.7), channel_id=1, replica_groups=mesh['walk'=16,'elec'=2] {'walk','elec'}, use_global_device_ids=true, to_apply=%region_6.0 | all-reduce | flops 3584 | bytes 28672 | tf_op jit(solution)/shard_map/psum | solution.py:96
  371.0 89.6 %all-reduce.11.cloned.1.call-done = (f32[2,256,32]{1,2,0:T(8,128)}, f32[2,256,256]{2,1,0:T(8,128)}, f32[2,32,256]{2,1,0:T(8,128)}) async-done(((f32[2,256,32]{1,2,0:T(8,128)}, f32[2,256,256]{2,1,0:T(8,128)}, f32[2,32,256]{2,1,0:T(8,128)}), (f32[2,256,32]{1,2,0:T(8,128)}, f32[2,256,256]{2,1,0:T(8,128)}, f32[2,32,256]{2,1,0:T(8,128)})) %all-reduce.11.cloned.1.call-update) | async-done | bytes 655376 | tf_op jit(solution)/shard_map/psum | solution.py:96
  (95 shorter events, 55.3 us)
Async XLA Ops:
  8.0 145.0 %copy-start = (bf16[256,3200]{1,0:T(8,128)(2,1)S(1)}, bf16[256,3200]{1,0:T(8,128)(2,1)}, u32[]{:S(2)}) copy-start(bf16[256,3200]{1,0:T(8,128)(2,1)} %param.19) | copy-start | bytes 4915204
  8.0 226.1 %all-reduce.9.cloned.1.call-start = ((), (), s32[]{:S(2)}) async-start(), calls=%async_computation.2 | async-start | bytes 393216
  12.1 1.5 copy-start.16
  41.9 21.2 %copy-start.18 = (f32[2,32,32]{2,1,0:T(8,128)S(1)}, f32[2,32,32]{2,1,0:T(8,128)}, u32[]{:S(2)}) copy-start(f32[2,32,32]{2,1,0:T(8,128)} %param.15) | copy-start | bytes 24580
  43.3 19.8 %copy-start.11 = (f32[6,32,200]{2,1,0:T(8,128)S(1)}, f32[6,32,200]{2,1,0:T(8,128)}, u32[]{:S(2)}) copy-start(f32[6,32,200]{2,1,0:T(8,128)} %copy.87) | copy-start | bytes 460804
  63.1 28.6 %copy-start.17 = (f32[2,256]{1,0:T(2,128)S(1)}, f32[2,256]{1,0:T(2,128)}, u32[]{:S(2)}) copy-start(f32[2,256]{1,0:T(2,128)} %param.18) | copy-start | bytes 6148
  63.1 28.6 %copy-start.12 = (f32[2,32,256]{2,1,0:T(8,128)S(1)}, f32[2,32,256]{2,1,0:T(8,128)}, u32[]{:S(2)}) copy-start(f32[2,32,256]{2,1,0:T(8,128)} %param.17) | copy-start | bytes 196612
  63.1 29.3 %copy-start.2 = (f32[2,256,256]{2,1,0:T(8,128)S(1)}, f32[2,256,256]{2,1,0:T(8,128)}, u32[]{:S(2)}) copy-start(f32[2,256,256]{2,1,0:T(8,128)} %param.16) | copy-start | bytes 1572868
  91.7 0.7 copy-start.7
  142.9 20.4 %copy-start.9 = (f32[6,32,100]{2,1,0:T(8,128)}, f32[6,32,100]{2,1,0:T(8,128)S(1)}, u32[]{:S(2)}) copy-start(f32[6,32,100]{2,1,0:T(8,128)S(1)} %copy.72) | copy-start | bytes 230404
  147.1 16.2 %copy-start.3 = (bf16[600,256]{1,0:T(8,128)(2,1)}, bf16[600,256]{1,0:T(8,128)(2,1)S(1)}, u32[]{:S(2)}) copy-start(bf16[600,256]{1,0:T(8,128)(2,1)S(1)} %convert_element_type.16) | copy-start | bytes 921604
  157.4 1.8 copy-start.1
  166.8 0.7 copy-start.4
  194.4 103.8 %reduce-scatter.4.cloned.1.call-start = ((), (), s32[]{:S(2)}) async-start(), calls=%async_computation.1 | async-start | bytes 3481600 | tf_op jit(solution)/shard_map/reduce_scatter | solution.py:53
  200.0 124.7 %all-reduce.13.cloned.1.call-start = ((), (), s32[]{:S(2)}) async-start(), calls=%async_computation.4 | async-start | bytes 802816 | tf_op jit(solution)/shard_map/psum | solution.py:99
  203.8 24.5 %copy-start.10 = (f32[6,32,100]{2,1,0:T(8,128)S(1)}, f32[6,32,100]{2,1,0:T(8,128)}, u32[]{:S(2)}) copy-start(f32[6,32,100]{2,1,0:T(8,128)} %copy-done.9) | copy-start | bytes 230404
  239.3 0.6 copy-start.5
  269.1 24.1 %copy-start.15 = (f32[1,32,32]{2,1,0:T(8,128)S(1)}, f32[1,32,32]{2,1,0:T(8,128)}, u32[]{:S(2)}) copy-start(f32[1,32,32]{2,1,0:T(8,128)} %fusion.39) | copy-start | bytes 12292
  269.1 24.7 %copy-start.8 = (f32[6,32,100]{2,1,0:T(8,128)S(1)}, f32[6,32,100]{2,1,0:T(8,128)}, u32[]{:S(2)}) copy-start(f32[6,32,100]{2,1,0:T(8,128)} %copy-done.7) | copy-start | bytes 230404
  269.1 25.2 %copy-start.14 = (f32[1,32,256]{2,1,0:T(8,128)S(1)}, f32[1,32,256]{2,1,0:T(8,128)}, u32[]{:S(2)}) copy-start(f32[1,32,256]{2,1,0:T(8,128)} %convolution_bitcast_fusion.2) | copy-start | bytes 98308
  269.1 27.1 %copy-start.6 = (f32[1,256,256]{2,1,0:T(8,128)S(1)}, f32[1,256,256]{2,1,0:T(8,128)}, u32[]{:S(2)}) copy-start(f32[1,256,256]{2,1,0:T(8,128)} %convolution_bitcast_fusion) | copy-start | bytes 786436
  269.1 28.0 %copy-start.13 = (f32[6,200,32]{1,2,0:T(8,128)S(1)}, f32[6,200,32]{1,2,0:T(8,128)}, u32[]{:S(2)}) copy-start(f32[6,200,32]{1,2,0:T(8,128)} %all-reduce.9.cloned.1.call-done) | copy-start | bytes 460804
  298.3 162.4 %all-reduce.11.cloned.1.call-start = ((), (), s32[]{:S(2)}) async-start(), calls=%async_computation.3 | async-start | bytes 1310720 | tf_op jit(solution)/shard_map/psum | solution.py:96
Sparse Core Ops, SparseCore 0:
  194.6 22.5 all-reduce.8
  298.4 26.2 all-reduce.12
  330.9 129.7 all-reduce.10
Sparse Core Ops, SparseCore 1:
  200.1 67.0 reduce-scatter.3
where the time goes:
time: 483 us; the launch traced here: 475 us
  matrix products  222 us (46%)
  waiting for transfers between devices  113 us (23%)
  blocking collectives  75.4 us (16%)
  local copies, waits for them, and re-layouts  35.1 us (7%)
  between operations  16.7 us (3%)
  other arithmetic  12.4 us (3%)
    dot_general x4, matrix products, layer_update(): jnp.einsum('wiep,pq->wieq', pairs, w_gate, precision=HI)  106 us
    psum x1, waiting for transfers between devices, on_device(): lax.psum((grad_in, grad_up, grad_gate, grad_mix, grad_msg, grad_bias), ('...  89.6 us
    dot_general x2, matrix products, layer_update(): jnp.einsum('wieq,weq->wiq', gates, s_all, precision=HI) / s_all.shape[1]  53 us
    psum x1, blocking collectives, on_device(): lax.psum((grad_in, grad_up, grad_gate, grad_mix, grad_msg, grad_bias), ('...  40.5 us
    all_gather x2, blocking collectives, on_device(): proj = lax.all_gather(local_proj, 'elec', axis=1, tiled=True)  27.8 us
    psum x1, waiting for transfers between devices, on_device(): grad_head = lax.psum(head_part, 'elec')  23.3 us
    dot_general x1, matrix products, embed_pairs(): return jnp.tanh(jnp.einsum('wcie,cp->wiep', feats, v_in, precision=HI))  19.8 us
    unnamed x47, local copies, waits for them, and re-layouts  17 us
  transfers between devices with their start and end apart: 4, of which 2 were waited for; matrix products, arithmetic and copies ran while one was open for 23% of the time, Pallas kernels for 0%

commit v1 on v0

v1 whole, which is shorter than its diff:
```python
import functools

import jax
import jax.numpy as jnp
from jax import lax
from jax.experimental import pallas as pl
from jax.experimental.pallas import tpu as pltpu
from jax.sharding import PartitionSpec as P

LAYERS = 2
PACK = 8
CHUNK = 5

HI = lax.Precision.HIGHEST
F32 = jnp.float32
BF16 = jnp.bfloat16


def split(x):
    high = x.astype(BF16)
    return high, (x - high.astype(F32)).astype(BF16)


def pair_kernel(groups, rows, xi_ref, xj_ref, v_ref, w_ref, proj_ref, fold_ref, pairs_ref, t0_ref, t1_ref, msg_ref):
    width = v_ref.shape[1]
    w_high, w_low = split(w_ref[...])
    acc = jnp.zeros((rows, width), F32)
    total = jnp.zeros((1, width), F32)
    for start in range(0, groups, CHUNK):
        for k in range(start, start + CHUNK):
            dx = xi_ref[0, :, 0:1] - xj_ref[0, k, 0:1, :]
            dy = xi_ref[0, :, 1:2] - xj_ref[0, k, 1:2, :]
            dz = xi_ref[0, :, 2:3] - xj_ref[0, k, 2:3, :]
            dist = jnp.sqrt(dx * dx + dy * dy + dz * dz + 1.0)
            pre = dx * v_ref[0:1, :] + dy * v_ref[1:2, :] + dz * v_ref[2:3, :] + dist * v_ref[3:4, :]
            pairs_ref[0, k] = jnp.tanh(pre)
        flat = pairs_ref[0, start : start + CHUNK].reshape(CHUNK * rows, width)
        high, low = split(flat)
        z = jnp.dot(high, w_high, preferred_element_type=F32)
        z = z + jnp.dot(low, w_high, preferred_element_type=F32)
        z = z + jnp.dot(high, w_low, preferred_element_type=F32)
        t = jnp.tanh(z)
        t0_ref[0, start : start + CHUNK] = t[:, :width].reshape(CHUNK, rows, width)
        t1_ref[0, start : start + CHUNK] = t[:, width:].reshape(CHUNK, rows, width)
        for k in range(start, start + CHUNK):
            row = proj_ref[0, k]
            acc = acc + t0_ref[0, k] * row
            total = total + row
    msg_ref[0] = jnp.dot(acc + total, fold_ref[...], precision=HI, preferred_element_type=F32)


def message_kernel(groups, rows, t_ref, proj_ref, fold_ref, msg_ref):
    width = t_ref.shape[3]
    acc = jnp.zeros((rows, width), F32)
    total = jnp.zeros((1, width), F32)
    for k in range(groups):
        row = proj_ref[0, k]
        acc = acc + t_ref[0, k] * row
        total = total + row
    msg_ref[0] = jnp.dot(acc + total, fold_ref[...], precision=HI, preferred_element_type=F32)


def back_kernel(groups, rows, pairs_ref, t_ref, proj_ref, dm_ref, dproj_ref, gate_ref, tiled_ref, dz_ref):
    width = t_ref.shape[3]

    @pl.when(pl.program_id(0) == 0)
    def _():
        gate_ref[...] = jnp.zeros_like(gate_ref)

    tiled_ref[...] = jnp.concatenate([dm_ref[0]] * PACK, axis=1)
    dims = (((0,), (0,)), ((), ()))
    for start in range(0, groups, CHUNK):
        for k in range(start, start + CHUNK):
            t = t_ref[0, k]
            both = tiled_ref[...] * (1.0 + t)
            dproj_ref[0, k] = jnp.sum(both, axis=0, keepdims=True)
            dz_ref[k - start] = both * (1.0 - t) * proj_ref[0, k]
        p_high, p_low = split(pairs_ref[0, start : start + CHUNK].reshape(CHUNK * rows, width))
        d_high, d_low = split(dz_ref[...].reshape(CHUNK * rows, width))
        part = lax.dot_general(p_high, d_high, dims, preferred_element_type=F32)
        part = part + lax.dot_general(p_low, d_high, dims, preferred_element_type=F32)
        part = part + lax.dot_general(p_high, d_low, dims, preferred_element_type=F32)
        gate_ref[...] += part


def whole(shape):
    return pl.BlockSpec(shape, lambda w: (0,) * len(shape))


def per_walker(shape):
    return pl.BlockSpec((1,) + shape, lambda w: (w,) + (0,) * len(shape))


PARAMS = pltpu.CompilerParams(vmem_limit_bytes=50 * 1024 * 1024)


def on_device(positions, targets, w_in, v_in, w_up, w_gate, w_mix, w_msg, bias, w_head):
    walk_size = lax.axis_size("walk")
    elec_size = lax.axis_size("elec")
    own, _, mine = positions.shape
    walkers = own * walk_size
    every = mine * elec_size
    features = v_in.shape[1]
    width = PACK * features
    groups = every // PACK
    rows = -(-mine // 8) * 8

    pos_all = lax.all_gather(positions, "elec", axis=2, tiled=True)
    me = lax.axis_index("elec")

    feats = jnp.concatenate(
        [pos_all, jnp.sqrt(jnp.sum(pos_all * pos_all, axis=1, keepdims=True) + 1.0)], axis=1
    )
    states_all = jnp.tanh(jnp.einsum("wci,ch->wih", feats, w_in, precision=HI))
    proj = jnp.einsum("wjh,hp->wjp", states_all, w_up[0], precision=HI)
    own_feats = lax.dynamic_slice_in_dim(feats, me * mine, mine, 2)
    states0 = lax.dynamic_slice_in_dim(states_all, me * mine, mine, 1)

    xi = jnp.pad(jnp.transpose(positions, (0, 2, 1)), ((0, 0), (0, rows - mine), (0, 0)))
    xj = jnp.transpose(pos_all.reshape(own, 3, groups, PACK), (0, 2, 1, 3))
    xj = jnp.repeat(xj, features, axis=3)
    v_tiled = jnp.tile(v_in, (1, PACK))
    eye = jnp.eye(PACK, dtype=F32)
    blocks = [
        (0.5 * eye[:, None, :, None] * w_gate[l][None, :, None, :]).reshape(width, width)
        for l in range(LAYERS)
    ]
    w_pair = jnp.concatenate(blocks, axis=1)
    fold = jnp.tile(jnp.eye(features, dtype=F32), (PACK, 1)) * (0.5 / every)

    big = jax.ShapeDtypeStruct((own, groups, rows, width), F32)
    small = jax.ShapeDtypeStruct((own, rows, features), F32)
    big_spec = per_walker((groups, rows, width))
    row_spec = per_walker((groups, 1, width))
    small_spec = per_walker((rows, features))

    def as_rows(p):
        return p.reshape(own, groups, 1, width)

    rows0 = as_rows(proj)
    pairs, t0, t1, msg = pl.pallas_call(
        functools.partial(pair_kernel, groups, rows),
        grid=(own,),
        out_shape=(big, big, big, small),
        in_specs=[
            per_walker((rows, 3)),
            per_walker((groups, 3, width)),
            whole((4, width)),
            whole((width, LAYERS * width)),
            row_spec,
            whole((width, features)),
        ],
        out_specs=(big_spec, big_spec, big_spec, small_spec),
        compiler_params=PARAMS,
    )(xi, xj, v_tiled, w_pair, rows0, fold)

    def update(h, message, layer):
        pre = jnp.einsum("wih,hk->wik", h, w_mix[layer], precision=HI)
        pre = pre + jnp.einsum("wiq,qk->wik", message, w_msg[layer], precision=HI) + bias[layer]
        return jnp.tanh(pre)

    msg0 = msg[:, :mine]
    act0 = update(states0, msg0, 0)
    states1 = act0 + states0
    local_proj = jnp.einsum("wjh,hp->wjp", states1, w_up[1], precision=HI)
    rows1 = as_rows(lax.all_gather(local_proj, "elec", axis=1, tiled=True))
    msg = pl.pallas_call(
        functools.partial(message_kernel, groups, rows),
        grid=(own,),
        out_shape=small,
        in_specs=[big_spec, row_spec, whole((width, features))],
        out_specs=small_spec,
        compiler_params=PARAMS,
    )(t1, rows1, fold)
    msg1 = msg[:, :mine]
    act1 = update(states1, msg1, 1)
    states2 = act1 + states1

    last = states2.reshape(-1, states2.shape[2]).astype(BF16)
    orbitals = jnp.dot(last, w_head, preferred_element_type=F32)
    flat_targets = targets.reshape(-1, targets.shape[2]).astype(F32)
    d_orb = (2.0 / walkers * (orbitals - flat_targets)).astype(BF16)
    d_states = lax.dot_general(d_orb, w_head, (((1,), (1,)), ((), ())), preferred_element_type=F32)
    d_states = d_states.reshape(states2.shape)
    head = lax.dot_general(d_orb, last, (((0,), (0,)), ((), ())), preferred_element_type=F32)
    head_part = lax.psum_scatter(head, "walk", scatter_dimension=0, tiled=True)

    def back(d_out, h, act, message, t, rows_l, layer):
        d_pre = d_out * (1.0 - act * act)
        g_bias = jnp.sum(d_pre, axis=(0, 1))
        g_mix = jnp.einsum("wih,wik->hk", h, d_pre, precision=HI)
        g_msg = jnp.einsum("wiq,wik->qk", message, d_pre, precision=HI)
        d_msg = jnp.einsum("wik,qk->wiq", d_pre, w_msg[layer], precision=HI) * (0.5 / every)
        d_msg = jnp.pad(d_msg, ((0, 0), (0, rows - mine), (0, 0)))
        d_rows, g_wide = pl.pallas_call(
            functools.partial(back_kernel, groups, rows),
            grid=(own,),
            out_shape=(
                jax.ShapeDtypeStruct((own, groups, 1, width), F32),
                jax.ShapeDtypeStruct((width, width), F32),
            ),
            in_specs=[big_spec, big_spec, row_spec, small_spec],
            out_specs=(row_spec, whole((width, width))),
            scratch_shapes=[pltpu.VMEM((rows, width), F32), pltpu.VMEM((CHUNK, rows, width), F32)],
            compiler_params=PARAMS,
        )(pairs, t, rows_l, d_msg)
        g_gate = 0.5 * sum(
            g_wide[k * features : (k + 1) * features, k * features : (k + 1) * features]
            for k in range(PACK)
        )
        d_proj = d_rows.reshape(own, every, features)
        d_own = lax.psum_scatter(d_proj, "elec", scatter_dimension=1, tiled=True)
        g_up = jnp.einsum("wjh,wjp->hp", h, d_own, precision=HI)
        d_in = d_out + jnp.einsum("wik,hk->wih", d_pre, w_mix[layer], precision=HI)
        d_in = d_in + jnp.einsum("wjp,hp->wjh", d_own, w_up[layer], precision=HI)
        return d_in, g_up, g_gate, g_mix, g_msg, g_bias

    d1, *g1 = back(d_states, states1, act1, msg1, t1, rows1, 1)
    d0, *g0 = back(d1, states0, act0, msg0, t0, rows0, 0)
    g_in = jnp.einsum("wci,wih->ch", own_feats, d0 * (1.0 - states0 * states0), precision=HI)
    return finish(head_part, g_in, *[jnp.stack([a, b]) for a, b in zip(g0, g1)])


def finish(head_part, *grads):
    return (lax.psum(head_part, "elec"),) + lax.psum(grads, ("walk", "elec"))


def solution(mesh):
    return jax.shard_map(
        on_device,
        mesh=mesh,
        in_specs=(P("walk", None, "elec"), P("walk", "elec", None)) + (P(),) * 8,
        out_specs=(P("walk", None),) + (P(),) * 6,
        check_vma=False,
    )
```

time: 483 us -> 385 us (0.80); the launches traced: 475 us -> 384 us
  matrix products: 222 us -> 41 us
  Pallas kernels: 0 us -> 66.4 us
  waiting for transfers between devices: 113 us -> 157 us
  blocking collectives: 75.4 us -> 60.5 us
    dot_general x28 -> x21, matrix products: 214 us -> 33.6 us  [the longest x2 5.61 us: back(): d_in = d_out + jnp.einsum('wik,hk->wih', d_pre, w_mix[layer], precision=HI)]
    pallas_call x0 -> x4, Pallas kernels: none -> 66.4 us  [the longest x2 32.2 us: back(): pl.pallas_call(functools.partial(back_kernel, groups, rows), grid=(own,),...]
    unnamed x5, waiting for transfers between devices: 0.07 us -> 21.9 us
    all_gather x2 -> x1, blocking collectives: 27.8 us -> 11.5 us  [on_device(): rows1 = as_rows(lax.all_gather(local_proj, 'elec', axis=1, tiled=True))]
    reduce_scatter x1, waiting for transfers between devices: 0.01 us -> 14.5 us  [on_device(): head_part = lax.psum_scatter(head, 'walk', scatter_dimension=0, tiled=True)]
    psum x2, waiting for transfers between devices: 113 us -> 121 us  [finish(): return (lax.psum(head_part, 'elec'),) + lax.psum(grads, ('walk', 'elec'))]
    reshape x1 -> x7, local copies, waits for them, and re-layouts: 1.99 us -> 7.28 us  [the longest x2 2.42 us: on_device(): xj = jnp.repeat(xj, features, axis=3)]
    unnamed x47 -> x61, local copies, waits for them, and re-layouts: 17 us -> 12 us
  transfers between devices with their start and end apart: 4 -> 4, of which waited for: 2 -> 4; matrix products, arithmetic and copies ran while one was open for 23% -> 6% of each run, Pallas kernels for 0% -> 4%
where the time goes in v1:
time: 385 us; the launch traced here: 384 us
  waiting for transfers between devices  157 us (41%)
  Pallas kernels  66.4 us (17%)
  blocking collectives  60.5 us (16%)
  matrix products  41 us (11%)
  local copies, waits for them, and re-layouts  33.8 us (9%)
  between operations  16.4 us (4%)
  other arithmetic  8.12 us (2%)
    psum x2, waiting for transfers between devices, finish(): return (lax.psum(head_part, 'elec'),) + lax.psum(grads, ('walk', 'elec'))  121 us
    psum x1, blocking collectives, finish(): return (lax.psum(head_part, 'elec'),) + lax.psum(grads, ('walk', 'elec'))  40.3 us
    pallas_call x2, Pallas kernels, back(): pl.pallas_call(functools.partial(back_kernel, groups, rows), grid=(own,),...  32.2 us
    pallas_call x1, Pallas kernels, on_device(): pl.pallas_call(functools.partial(pair_kernel, groups, rows), grid=(own,),...  26.3 us
    unnamed x5, waiting for transfers between devices  21.9 us
    reduce_scatter x1, waiting for transfers between devices, on_device(): head_part = lax.psum_scatter(head, 'walk', scatter_dimension=0, tiled=True)  14.5 us
    unnamed x61, local copies, waits for them, and re-layouts  12 us
    all_gather x1, blocking collectives, on_device(): rows1 = as_rows(lax.all_gather(local_proj, 'elec', axis=1, tiled=True))  11.5 us
  transfers between devices with their start and end apart: 4, of which 4 were waited for; matrix products, arithmetic and copies ran while one was open for 6% of the time, Pallas kernels for 4%

profile of v1, /device:TPU:0, one launch (start us, length us, event | category | flops | bytes accessed | tf_op | source)
XLA Modules:
  0.0 383.7 jit_solution(10395848295846460275)
XLA Ops:
  9.1 8.7 %all_gather.6 = f32[6,3,200]{0,1,2:T(4,128)S(1)} all-gather(f32[6,3,100]{0,1,2:T(4,128)S(1)} %copy.95), channel_id=1, replica_groups=mesh['walk'=16,'elec'=2] {'elec'}, dimensions={2}, use_global_device_ids=true | all-gather | bytes 21600 | tf_op jit(solution)/shard_map/all_gather | solution.py:108
  25.0 2.2 mul.108
  30.9 2.1 reshape.94
  35.1 26.3 %shard_map.153 = (f32[6,25,104,256]{3,2,1,0:T(8,128)}, f32[6,25,104,256]{3,2,1,0:T(8,128)}, f32[6,25,104,256]{3,2,1,0:T(8,128)}, f32[6,104,32]{2,1,0:T(8,128)S(1)}) custom-call(f32[6,104,3]{2,1,0:T(8,128)S(1)} %pad.11.xi_ref, f32[6,25,3,256]{3,2,1,0:T(4,128)S(1)} %copy.102.xj_ref, f32[4,256]{1,0:T(4,128)S(1)} %tile.9.v_ref, ...), custom_call_target="tpu_custom_call" | custom-call | tf_op jit(solution)/shard_map/pallas_call | solution.py:141
  63.0 3.2 dynamic-slice_add_fusion
  67.1 11.5 %all_gather.7 = f32[6,200,32]{2,0,1:T(8,128)S(1)} all-gather(f32[6,100,32]{2,0,1:T(8,128)S(1)} %copy.105), channel_id=1, replica_groups=mesh['walk'=16,'elec'=2] {'elec'}, dimensions={1}, use_global_device_ids=true | all-gather | bytes 230400 | tf_op jit(solution)/shard_map/all_gather | solution.py:166
  81.0 7.9 %shard_map.154 = f32[6,104,32]{2,1,0:T(8,128)S(1)} custom-call(f32[6,25,104,256]{3,2,1,0:T(8,128)} %get-tuple-element.16.t_ref, f32[6,25,1,256]{3,2,1,0:T(1,128)S(1)} %reshape.122.proj_ref, f32[256,32]{1,0:T(8,128)S(1)} %bitcast.116), custom_call_target="tpu_custom_call" | custom-call | tf_op jit(solution)/shard_map/pallas_call | solution.py:167
  91.9 5.7 %reshape.100 = f32[600,3200]{1,0:T(8,128)} reshape(bf16[6,100,3200]{2,1,0:T(8,128)(2,1)} %param.11) | data formatting | bytes 11520000 | tf_op jit(solution)/shard_map/convert_element_type | solution.py:181
  97.6 4.4 %multiply_convert_fusion = bf16[600,3200]{1,0:T(8,128)(2,1)S(1)} fusion(f32[600,3200]{1,0:T(8,128)} %reshape.100, bf16[600,256]{1,0:T(8,128)(2,1)S(1)} %copy-done.12, bf16[256,3200]{1,0:T(8,128)(2,1)S(1)} %copy-done), kind=kOutput, calls=%fused_computation | convolution fusion | flops 988800000 | bytes 13465600 | tf_op jit(solution)/shard_map/dot_general | solution.py:180
  103.8 2.1 fusion.68
  109.3 16.0 %shard_map.155 = (f32[6,25,1,256]{3,2,1,0:T(1,128)S(1)}, f32[256,256]{1,0:T(8,128)S(1)}) custom-call(f32[6,25,104,256]{3,2,1,0:T(8,128)} %get-tuple-element.17.pairs_ref, f32[6,25,104,256]{3,2,1,0:T(8,128)} %get-tuple-element.16.t_ref, f32[6,25,1,256]{3,2,1,0:T(1,128)S(1)} %reshape.122.proj_ref, f32[6,104,32]{2,1,0:T(8,128)S(1)} %pad.12.dm_ref), custom_call_target="tpu_custom_call" | custom-call | tf_op jit(solution)/shard_map/pallas_call | solution.py:195
  126.7 5.3 %fusion.67 = f32[3200,256]{1,0:T(8,128)} fusion(bf16[600,3200]{1,0:T(8,128)(2,1)} %copy-done.9, bf16[600,256]{1,0:T(8,128)(2,1)S(1)} %copy-done.12), kind=kOutput, calls=%fused_computation.104 | convolution fusion | flops 983040000 | bytes 7424000 | tf_op jit(solution)/shard_map/dot_general | solution.py:185
  134.7 2.0 convolution_bitcast_fusion
  136.7 21.8 %all-reduce.12.cloned.1.call-done = f32[6,200,32]{2,1,0:T(8,128)} async-done(((f32[6,200,32]{2,1,0:T(8,128)}), f32[6,200,32]{2,1,0:T(8,128)}) %all-reduce.12.cloned.1.call-update) | async-done | bytes 153616
  160.1 3.2 fusion.64
  164.0 16.2 %shard_map.156 = (f32[6,25,1,256]{3,2,1,0:T(1,128)S(1)}, f32[256,256]{1,0:T(8,128)S(1)}) custom-call(f32[6,25,104,256]{3,2,1,0:T(8,128)} %get-tuple-element.17.pairs_ref, f32[6,25,104,256]{3,2,1,0:T(8,128)} %get-tuple-element.19.t_ref, f32[6,25,1,256]{3,2,1,0:T(1,128)S(1)} %reshape.121.proj_ref, f32[6,104,32]{2,1,0:T(8,128)S(1)} %pad.13.dm_ref), custom_call_target="tpu_custom_call" | custom-call | tf_op jit(solution)/shard_map/pallas_call | solution.py:195
  183.0 1.8 pad_maximum_fusion.1
  185.5 14.5 %reduce-scatter.4.cloned.1.call-done = f32[200,256]{1,0:T(8,128)} async-done(((f32[3200,256]{1,0:T(8,128)}), f32[200,256]{1,0:T(8,128)}) %reduce-scatter.4.cloned.1.call-update) | async-done | bytes 204816 | tf_op jit(solution)/shard_map/reduce_scatter | solution.py:186
  202.4 32.0 %all-reduce.16.cloned.1.call-done = (f32[200,256]{1,0:T(8,128)}, f32[6,200,32]{2,1,0:T(8,128)}) async-done(((f32[200,256]{1,0:T(8,128)}, f32[6,200,32]{2,1,0:T(8,128)}), (f32[200,256]{1,0:T(8,128)}, f32[6,200,32]{2,1,0:T(8,128)})) %all-reduce.16.cloned.1.call-update) | async-done | bytes 358416 | tf_op jit(solution)/shard_map/psum | solution.py:225
  236.1 2.5 fusion.17
  239.3 2.4 fusion.6
  242.2 40.3 %all-reduce.5 = (f32[4,256]{1,0:T(4,128)}, f32[2,32,32]{2,1,0:T(8,128)}, f32[2,256]{1,0:T(2,128)}) all-reduce(f32[4,256]{1,0:T(4,128)S(1)} %convolution_bitcast_fusion.6, f32[2,32,32]{2,1,0:T(8,128)S(1)} %pad_maximum_fusion.4, f32[2,256]{1,0:T(2,128)S(1)} %pad_maximum_fusion.7), channel_id=1, replica_groups=mesh['walk'=16,'elec'=2] {'walk','elec'}, use_global_device_ids=true, to_apply=%region_5.6 | all-reduce | flops 3584 | bytes 28672 | tf_op jit(solution)/shard_map/psum | solution.py:225
  282.5 88.6 %all-reduce.14.cloned.1.call-done = (f32[2,256,32]{1,2,0:T(8,128)}, f32[2,256,256]{2,1,0:T(8,128)}, f32[2,32,256]{2,1,0:T(8,128)}) async-done(((f32[2,256,32]{1,2,0:T(8,128)}, f32[2,256,256]{2,1,0:T(8,128)}, f32[2,32,256]{2,1,0:T(8,128)}), (f32[2,256,32]{1,2,0:T(8,128)}, f32[2,256,256]{2,1,0:T(8,128)}, f32[2,32,256]{2,1,0:T(8,128)})) %all-reduce.14.cloned.1.call-update) | async-done | bytes 655376 | tf_op jit(solution)/shard_map/psum | solution.py:225
  373.2 1.9 copy.146
  (121 shorter events, 44.6 us)
Async XLA Ops:
  8.0 89.6 %copy-start = (bf16[256,3200]{1,0:T(8,128)(2,1)S(1)}, bf16[256,3200]{1,0:T(8,128)(2,1)}, u32[]{:S(2)}) copy-start(bf16[256,3200]{1,0:T(8,128)(2,1)} %param.19) | copy-start | bytes 4915204
  8.0 12.0 %copy-start.22 = (f32[4,256]{1,0:T(4,128)S(1)}, f32[4,256]{1,0:T(4,128)}, u32[]{:S(2)}) copy-start(f32[4,256]{1,0:T(4,128)} %param.12) | copy-start | bytes 12292
  8.0 14.3 %copy-start.13 = (f32[2,256,32]{1,2,0:T(8,128)S(1)}, f32[2,256,32]{1,2,0:T(8,128)}, u32[]{:S(2)}) copy-start(f32[2,256,32]{1,2,0:T(8,128)} %param.14) | copy-start | bytes 196612
  8.0 150.5 %all-reduce.12.cloned.1.call-start = ((), (), s32[]{:S(2)}) async-start(), calls=%async_computation.2 | async-start | bytes 1228800
  18.3 3.0 copy-start.18
  20.0 3.7 copy-start.21
  30.9 4.2 %copy-start.11 = (f32[6,3,100]{1,2,0:T(8,128)S(1)}, f32[6,3,100]{1,2,0:T(8,128)}, u32[]{:S(2)}) copy-start(f32[6,3,100]{1,2,0:T(8,128)} %copy.98) | copy-start | bytes 21604
  33.3 28.1 %copy-start.15 = (f32[2,32,256]{2,1,0:T(8,128)S(1)}, f32[2,32,256]{2,1,0:T(8,128)}, u32[]{:S(2)}) copy-start(f32[2,32,256]{2,1,0:T(8,128)} %param.17) | copy-start | bytes 196612
  66.1 68.5 %copy-start.4 = (f32[6,100,256]{2,1,0:T(8,128)}, f32[6,100,256]{2,1,0:T(8,128)S(1)}, u32[]{:S(2)}) copy-start(f32[6,100,256]{2,1,0:T(8,128)S(1)} %get-tuple-element.41) | copy-start | bytes 1843204
  81.0 7.9 %copy-start.16 = (f32[2,32,256]{2,1,0:T(8,128)S(1)}, f32[2,32,256]{2,1,0:T(8,128)}, u32[]{:S(2)}) copy-start(f32[2,32,256]{2,1,0:T(8,128)} %param.17) | copy-start | bytes 196612
  81.0 8.6 %copy-start.10 = (f32[2,256,256]{2,1,0:T(8,128)S(1)}, f32[2,256,256]{2,1,0:T(8,128)}, u32[]{:S(2)}) copy-start(f32[2,256,256]{2,1,0:T(8,128)} %param.16) | copy-start | bytes 1572868
  81.0 8.6 %copy-start.23 = (f32[1,256]{1,0:T(1,128)S(1)}, f32[1,256]{1,0:T(1,128)}, u32[]{:S(2)}) copy-start(f32[1,256]{1,0:T(1,128)} %get-tuple-element.39) | copy-start | bytes 3076
  91.9 5.7 %copy-start.12 = (bf16[600,256]{1,0:T(8,128)(2,1)S(1)}, bf16[600,256]{1,0:T(8,128)(2,1)}, u32[]{:S(2)}) copy-start(bf16[600,256]{1,0:T(8,128)(2,1)} %convert_element_type.28) | copy-start | bytes 921604
  105.9 2.6 copy-start.17
  108.6 26.1 %copy-start.7 = (f32[6,100,256]{2,1,0:T(8,128)}, f32[6,100,256]{2,1,0:T(8,128)S(1)}, u32[]{:S(2)}) copy-start(f32[6,100,256]{2,1,0:T(8,128)S(1)} %get-tuple-element.34) | copy-start | bytes 1843204
  126.7 73.3 %reduce-scatter.4.cloned.1.call-start = ((), (), s32[]{:S(2)}) async-start(), calls=%async_computation.1 | async-start | bytes 3481600 | tf_op jit(solution)/shard_map/reduce_scatter | solution.py:186
  132.0 26.5 %copy-start.14 = (f32[2,256,32]{1,2,0:T(8,128)S(1)}, f32[2,256,32]{1,2,0:T(8,128)}, u32[]{:S(2)}) copy-start(f32[2,256,32]{1,2,0:T(8,128)} %param.14) | copy-start | bytes 196612
  132.1 102.4 %all-reduce.16.cloned.1.call-start = ((), (), s32[]{:S(2)}) async-start(), calls=%async_computation.4 | async-start | bytes 1638400 | tf_op jit(solution)/shard_map/psum | solution.py:225
  163.3 21.5 %copy-start.6 = (f32[6,100,256]{2,1,0:T(8,128)}, f32[6,100,256]{2,1,0:T(8,128)S(1)}, u32[]{:S(2)}) copy-start(f32[6,100,256]{2,1,0:T(8,128)S(1)} %get-tuple-element.32) | copy-start | bytes 1843204
  164.0 17.7 %copy-start.3 = (f32[6,200,256]{2,1,0:T(8,128)S(1)}, f32[6,200,256]{2,1,0:T(8,128)}, u32[]{:S(2)}) copy-start(f32[6,200,256]{2,1,0:T(8,128)} %copy-done.2) | copy-start | bytes 3686404
  183.0 17.7 %copy-start.5 = (f32[6,100,256]{2,1,0:T(8,128)S(1)}, f32[6,100,256]{2,1,0:T(8,128)}, u32[]{:S(2)}) copy-start(f32[6,100,256]{2,1,0:T(8,128)} %copy-done.4) | copy-start | bytes 1843204
  200.0 171.0 %all-reduce.14.cloned.1.call-start = ((), (), s32[]{:S(2)}) async-start(), calls=%async_computation.3 | async-start | bytes 1310720 | tf_op jit(solution)/shard_map/psum | solution.py:225
  239.3 131.8 %copy-start.20 = (f32[200,256]{1,0:T(8,128)S(1)}, f32[200,256]{1,0:T(8,128)}, u32[]{:S(2)}) copy-start(f32[200,256]{1,0:T(8,128)} %get-tuple-element.46) | copy-start | bytes 614404
  239.3 137.3 %copy-start.1 = (bf16[256,3200]{1,0:T(8,128)(2,1)S(1)}, bf16[256,3200]{1,0:T(8,128)(2,1)}, u32[]{:S(2)}) copy-start(bf16[256,3200]{1,0:T(8,128)(2,1)} %param.19) | copy-start | bytes 4915204
  (7 other events, 12.5 us)
Sparse Core Ops, SparseCore 0:
  126.8 31.6 all-reduce.11
  200.2 34.2 all-reduce.15
  241.4 129.5 all-reduce.13
Sparse Core Ops, SparseCore 1:
  132.1 67.8 reduce-scatter.3

commit v2 on v1

--- a/solution.py
+++ b/solution.py
@@ -83,6 +83,42 @@
         gate_ref[...] += part
 
 
+def swap(x, axis, bit):
+    size = lax.axis_size(axis)
+    return lax.ppermute(x, axis, [(i, i ^ bit) for i in range(size)])
+
+
+def bits_of(axis):
+    return [1 << k for k in range(lax.axis_size(axis).bit_length() - 1)]
+
+
+def sum_over(x, axis):
+    for bit in bits_of(axis):
+        x = x + swap(x, axis, bit)
+    return x
+
+
+def sum_scatter(x, axis):
+    me = lax.axis_index(axis)
+    for bit in bits_of(axis):
+        mine = (me // bit) % 2
+        x = x.reshape((x.shape[0] // 2, 2) + x.shape[1:])
+        keep = lax.dynamic_index_in_dim(x, mine, 1, keepdims=False)
+        send = lax.dynamic_index_in_dim(x, 1 - mine, 1, keepdims=False)
+        x = keep + swap(send, axis, bit)
+    return x
+
+
+def gather(x, axis):
+    me = lax.axis_index(axis)
+    for bit in reversed(bits_of(axis)):
+        first = (me // bit) % 2 == 0
+        other = swap(x, axis, bit)
+        pair = jnp.stack([jnp.where(first, x, other), jnp.where(first, other, x)], axis=1)
+        x = pair.reshape((pair.shape[0] * 2,) + x.shape[1:])
+    return x
+
+
 def whole(shape):
     return pl.BlockSpec(shape, lambda w: (0,) * len(shape))
 
@@ -105,7 +141,7 @@
     groups = every // PACK
     rows = -(-mine // 8) * 8
 
-    pos_all = lax.all_gather(positions, "elec", axis=2, tiled=True)
+    pos_all = jnp.moveaxis(gather(positions[None], "elec"), 0, 2).reshape(own, 3, every)
     me = lax.axis_index("elec")
 
     feats = jnp.concatenate(
@@ -163,7 +199,7 @@
     act0 = update(states0, msg0, 0)
     states1 = act0 + states0
     local_proj = jnp.einsum("wjh,hp->wjp", states1, w_up[1], precision=HI)
-    rows1 = as_rows(lax.all_gather(local_proj, "elec", axis=1, tiled=True))
+    rows1 = as_rows(jnp.moveaxis(gather(local_proj[None], "elec"), 0, 1))
     msg = pl.pallas_call(
         functools.partial(message_kernel, groups, rows),
         grid=(own,),
@@ -208,8 +244,8 @@
             g_wide[k * features : (k + 1) * features, k * features : (k + 1) * features]
             for k in range(PACK)
         )
-        d_proj = d_rows.reshape(own, every, features)
-        d_own = lax.psum_scatter(d_proj, "elec", scatter_dimension=1, tiled=True)
+        d_proj = d_rows.reshape(own, elec_size, mine, features)
+        d_own = sum_scatter(jnp.moveaxis(d_proj, 1, 0), "elec")[0]
         g_up = jnp.einsum("wjh,wjp->hp", h, d_own, precision=HI)
         d_in = d_out + jnp.einsum("wik,hk->wih", d_pre, w_mix[layer], precision=HI)
         d_in = d_in + jnp.einsum("wjp,hp->wjh", d_own, w_up[layer], precision=HI)
@@ -222,7 +258,20 @@
 
 
 def finish(head_part, *grads):
-    return (lax.psum(head_part, "elec"),) + lax.psum(grads, ("walk", "elec"))
+    size = lax.axis_size("walk")
+    width = grads[0].shape[-1]
+    flat = jnp.concatenate([g.reshape(-1, width) for g in grads])
+    count = flat.shape[0]
+    block = -(-count // (8 * size)) * 8
+    flat = jnp.pad(flat, ((0, block * size - count), (0, 0))).reshape(size, block, width)
+    flat = gather(sum_over(sum_scatter(flat, "walk"), "elec"), "walk").reshape(-1, width)
+    outs = []
+    start = 0
+    for g in grads:
+        rows = g.size // width
+        outs.append(flat[start : start + rows].reshape(g.shape))
+        start += rows
+    return (sum_over(head_part, "elec"),) + tuple(outs)
 
 
 def solution(mesh):

time: 385 us -> 217 us (0.56)
  waiting for transfers between devices: 157 us -> 38.4 us
  blocking collectives: 60.5 us -> 0 us
  starting transfers between devices: 0.38 us -> 17.2 us
    psum x2 -> x0, waiting for transfers between devices: 121 us -> none  [finish(): return (lax.psum(head_part, 'elec'),) + lax.psum(grads, ('walk', 'elec'))]
    psum x1 -> x0, blocking collectives: 40.3 us -> none  [finish(): return (lax.psum(head_part, 'elec'),) + lax.psum(grads, ('walk', 'elec'))]
    ppermute x0 -> x14, waiting for transfers between devices: none -> 38.3 us  [swap(): return lax.ppermute(x, axis, [(i, i ^ bit) for i in range(size)])]
    unnamed x5 -> x1, waiting for transfers between devices: 21.9 us -> 0.04 us
    all_gather x2 -> x0, blocking collectives: 20.2 us -> none  [the longest x1 11.5 us: on_device(): rows1 = as_rows(lax.all_gather(local_proj, 'elec', axis=1, tiled=True))]
    ppermute x0 -> x14, starting transfers between devices: none -> 17.1 us  [swap(): return lax.ppermute(x, axis, [(i, i ^ bit) for i in range(size)])]
    reduce_scatter x1, waiting for transfers between devices: 14.5 us -> 0.01 us  [on_device(): head_part = lax.psum_scatter(head, 'walk', scatter_dimension=0, tiled=True)]
    unnamed x61 -> x70, local copies, waits for them, and re-layouts: 12 us -> 4 us
  transfers between devices with their start and end apart: 4 -> 15, of which waited for: 4 -> 11; matrix products, arithmetic and copies ran while one was open for 6% -> 17% of each run, Pallas kernels for 4% -> 8%
where the time goes in v2:
time: 217 us; the launch traced here: 216 us
  Pallas kernels  66.9 us (31%)
  matrix products  38.6 us (18%)
  waiting for transfers between devices  38.4 us (18%)
  local copies, waits for them, and re-layouts  32.2 us (15%)
  starting transfers between devices  17.2 us (8%)
  between operations  14.9 us (7%)
  other arithmetic  8.01 us (4%)
    ppermute x14, waiting for transfers between devices, swap(): return lax.ppermute(x, axis, [(i, i ^ bit) for i in range(size)])  38.3 us
    pallas_call x2, Pallas kernels, back(): pl.pallas_call(functools.partial(back_kernel, groups, rows), grid=(own,),...  32.8 us
    pallas_call x1, Pallas kernels, on_device(): pl.pallas_call(functools.partial(pair_kernel, groups, rows), grid=(own,),...  26.1 us
    ppermute x14, starting transfers between devices, swap(): return lax.ppermute(x, axis, [(i, i ^ bit) for i in range(size)])  17.1 us
    pallas_call x1, Pallas kernels, on_device(): pl.pallas_call(functools.partial(message_kernel, groups, rows), grid=(own...  8.11 us
    convert_element_type x1, local copies, waits for them, and re-layouts, on_device(): flat_targets = targets.reshape(-1, targets.shape[2]).astype(F32)  5.6 us
    dot_general x2, matrix products, back(): d_in = d_in + jnp.einsum('wjp,hp->wjh', d_own, w_up[layer], precision=HI)  4.94 us
    dot_general x1, matrix products, on_device(): orbitals = jnp.dot(last, w_head, preferred_element_type=F32)  4.51 us
  transfers between devices with their start and end apart: 15, of which 11 were waited for; matrix products, arithmetic and copies ran while one was open for 17% of the time, Pallas kernels for 8%

profile of v2, /device:TPU:0, one launch (start us, length us, event | category | flops | bytes accessed | tf_op | source)
XLA Modules:
  0.0 216.3 jit_solution(13779995545074884407)
XLA Ops:
  7.2 3.0 %collective-permute-start = (f32[1,6,3,100]{3,2,1,0:T(4,128)}, f32[1,6,3,100]{3,2,1,0:T(4,128)S(1)}, u32[]{:S(2)}, u32[]{:S(2)}) collective-permute-start(f32[1,6,3,100]{3,2,1,0:T(4,128)} %bitcast.239), channel_id=1, source_target_pairs={{0,1},{1,0},{2,3},{3,2},{4,5},{5,4},{6,7},{7,6},{8,9},{9,8},{10,11... | collective-permute-start | bytes 21608 | tf_op jit(solution)/shard_map/ppermute | solution.py:88
  22.7 2.7 %reshape.164 = f32[6,25,3,256]{3,1,2,0:T(8,128)} reshape(f32[6,25,3,8,32]{4,3,1,2,0:T(8,128)} %broadcast_in_dim.13) | data formatting | bytes 921600 | tf_op jit(solution)/shard_map/reshape | solution.py:157
  27.0 26.1 %shard_map.153 = (f32[6,25,104,256]{3,2,1,0:T(8,128)}, f32[6,25,104,256]{3,2,1,0:T(8,128)}, f32[6,25,104,256]{3,2,1,0:T(8,128)}, f32[6,104,32]{2,1,0:T(8,128)S(1)}) custom-call(f32[6,104,3]{2,1,0:T(8,128)S(1)} %pad.15.xi_ref, f32[6,25,3,256]{3,2,1,0:T(4,128)S(1)} %copy.166.xj_ref, f32[4,256]{1,0:T(4,128)S(1)} %tile.9.v_ref, ...), custom_call_target="tpu_custom_call" | custom-call | tf_op jit(solution)/shard_map/pallas_call | solution.py:177
  56.2 5.6 %reshape.184 = f32[600,3200]{1,0:T(8,128)} reshape(bf16[6,100,3200]{2,1,0:T(8,128)(2,1)} %param.11) | data formatting | bytes 11520000 | tf_op jit(solution)/shard_map/convert_element_type | solution.py:217
  64.3 8.1 %shard_map.154 = f32[6,104,32]{2,1,0:T(8,128)S(1)} custom-call(f32[6,25,104,256]{3,2,1,0:T(8,128)} %get-tuple-element.16.t_ref, f32[6,25,1,256]{3,2,1,0:T(1,128)S(1)} %reshape.200.proj_ref, f32[256,32]{1,0:T(8,128)S(1)} %bitcast.218), custom_call_target="tpu_custom_call" | custom-call | tf_op jit(solution)/shard_map/pallas_call | solution.py:203
  76.5 4.5 %multiply_convert_fusion = bf16[600,3200]{1,0:T(8,128)(2,1)S(1)} fusion(f32[600,3200]{1,0:T(8,128)} %reshape.184, bf16[600,256]{1,0:T(8,128)(2,1)} %convert_element_type.30, bf16[256,3200]{1,0:T(8,128)(2,1)S(1)} %copy-done), kind=kOutput, calls=%fused_computation | convolution fusion | flops 988800000 | bytes 13465600 | tf_op jit(solution)/shard_map/dot_general | solution.py:216
  82.8 2.1 fusion.60
  90.2 2.0 convolution_bitcast_fusion
  92.1 3.2 %fusion.59 = f32[3200,256]{1,0:T(8,128)} fusion(bf16[600,3200]{1,0:T(8,128)(2,1)S(1)} %copy-done.8, bf16[600,256]{1,0:T(8,128)(2,1)S(1)} %copy-done.15), kind=kOutput, calls=%fused_computation.130 | convolution fusion | flops 983040000 | bytes 7424000 | tf_op jit(solution)/shard_map/dot_general | solution.py:221
  95.4 16.2 %shard_map.155 = (f32[6,25,1,256]{3,2,1,0:T(1,128)S(1)}, f32[256,256]{1,0:T(8,128)S(1)}) custom-call(f32[6,25,104,256]{3,2,1,0:T(8,128)} %get-tuple-element.17.pairs_ref, f32[6,25,104,256]{3,2,1,0:T(8,128)} %get-tuple-element.16.t_ref, f32[6,25,1,256]{3,2,1,0:T(1,128)S(1)} %reshape.200.proj_ref, f32[6,104,32]{2,1,0:T(8,128)S(1)} %pad.16.dm_ref), custom_call_target="tpu_custom_call" | custom-call | tf_op jit(solution)/shard_map/pallas_call | solution.py:231
  112.4 2.0 collective-permute-start.3
  117.1 3.3 %fusion.56 = (f32[256]{0:T(256)}, f32[6,100,256]{2,1,0:T(8,128)S(1)}, f32[6,100,256]{2,1,0:T(8,128)}) fusion(f32[6,100,256]{2,1,0:T(8,128)S(1)} %copy-done.9, f32[6,100,256]{2,1,0:T(8,128)} %convolution_add_fusion.1, f32[2,256,32]{1,2,0:T(8,128)S(1)} %copy-done.19, f32[1,6,100,32]{2,3,1,0:T(8,128)S(1)} %collective-permute-done.3, ...), kind=kOutput, calls=%fused_computation.127 | convolution fusion | flops 59769344 | bytes 2712576 | tf_op jit(solution)/shard_map/wjp,hp->wjh/dot_general | solution.py:251
  121.7 1.9 convolution_bitcast_fusion.1
  124.3 16.5 %shard_map.156 = (f32[6,25,1,256]{3,2,1,0:T(1,128)S(1)}, f32[256,256]{1,0:T(8,128)S(1)}) custom-call(f32[6,25,104,256]{3,2,1,0:T(8,128)} %get-tuple-element.17.pairs_ref, f32[6,25,104,256]{3,2,1,0:T(8,128)} %get-tuple-element.19.t_ref, f32[6,25,1,256]{3,2,1,0:T(1,128)S(1)} %reshape.199.proj_ref, f32[6,104,32]{2,1,0:T(8,128)S(1)} %pad.17.dm_ref), custom_call_target="tpu_custom_call" | custom-call | tf_op jit(solution)/shard_map/pallas_call | solution.py:231
  144.6 2.8 %convolution_add_fusion = f32[6,100,256]{2,1,0:T(8,128)} fusion(f32[6,100,256]{2,1,0:T(8,128)} %get-tuple-element.97, f32[6,100,256]{2,1,0:T(8,128)S(1)} %get-tuple-element.68, f32[2,256,256]{2,1,0:T(8,128)} %param.16), kind=kOutput, calls=%fused_computation.2 | convolution fusion | flops 472012800 | bytes 2129920 | tf_op jit(solution)/shard_map/wik,hk->wih/dot_general | solution.py:250
  159.3 5.3 %collective-permute-done.6 = f32[4,48,256]{2,1,0:T(8,128)S(1)} collective-permute-done((f32[4,48,256]{2,1,0:T(8,128)S(1)}, f32[4,48,256]{2,1,0:T(8,128)S(1)}, u32[]{:S(2)}, u32[]{:S(2)}) %collective-permute-start.6) | collective-permute-done | bytes 196640 | tf_op jit(solution)/shard_map/ppermute | solution.py:88
  166.4 2.9 %collective-permute-done.7 = f32[2,48,256]{2,1,0:T(8,128)S(1)} collective-permute-done((f32[2,48,256]{2,1,0:T(8,128)S(1)}, f32[2,48,256]{2,1,0:T(8,128)S(1)}, u32[]{:S(2)}, u32[]{:S(2)}) %collective-permute-start.7) | collective-permute-done | bytes 98336 | tf_op jit(solution)/shard_map/ppermute | solution.py:88
  169.4 2.7 %collective-permute-start.8 = (f32[1,48,256]{2,1,0:T(8,128)S(1)}, f32[1,48,256]{2,1,0:T(8,128)S(1)}, u32[]{:S(2)}, u32[]{:S(2)}) collective-permute-start(f32[1,48,256]{2,1,0:T(8,128)S(1)} %constant_dynamic-slice_fusion), channel_id=1, source_target_pairs={{0,16},{2,18},{4,20},{6,22},{8,24},{10,26},{12,28},{14,30},{16,0},... | collective-permute-start | bytes 147464 | tf_op jit(solution)/shard_map/ppermute | solution.py:88
  172.1 4.4 %collective-permute-done.8 = f32[1,48,256]{2,1,0:T(8,128)S(1)} collective-permute-done((f32[1,48,256]{2,1,0:T(8,128)S(1)}, f32[1,48,256]{2,1,0:T(8,128)S(1)}, u32[]{:S(2)}, u32[]{:S(2)}) %collective-permute-start.8) | collective-permute-done | bytes 49184 | tf_op jit(solution)/shard_map/ppermute | solution.py:88
  176.8 3.9 %collective-permute-done.9 = f32[1,48,256]{2,1,0:T(8,128)S(1)} collective-permute-done((f32[1,48,256]{2,1,0:T(8,128)S(1)}, f32[1,48,256]{2,1,0:T(8,128)S(1)}, u32[]{:S(2)}, u32[]{:S(2)}) %collective-permute-start.9) | collective-permute-done | bytes 49184 | tf_op jit(solution)/shard_map/ppermute | solution.py:88
  181.4 4.4 %collective-permute-done.10 = f32[1,48,256]{2,1,0:T(8,128)S(1)} collective-permute-done((f32[1,48,256]{2,1,0:T(8,128)S(1)}, f32[1,48,256]{2,1,0:T(8,128)S(1)}, u32[]{:S(2)}, u32[]{:S(2)}) %collective-permute-start.10) | collective-permute-done | bytes 49184 | tf_op jit(solution)/shard_map/ppermute | solution.py:88
  187.2 3.3 %collective-permute-done.11 = f32[2,48,256]{2,1,0:T(8,128)S(1)} collective-permute-done((f32[2,48,256]{2,1,0:T(8,128)S(1)}, f32[2,48,256]{2,1,0:T(8,128)S(1)}, u32[]{:S(2)}, u32[]{:S(2)}) %collective-permute-start.11) | collective-permute-done | bytes 98336 | tf_op jit(solution)/shard_map/ppermute | solution.py:88
  192.0 4.4 %collective-permute-done.12 = f32[4,48,256]{2,1,0:T(8,128)S(1)} collective-permute-done((f32[4,48,256]{2,1,0:T(8,128)S(1)}, f32[4,48,256]{2,1,0:T(8,128)S(1)}, u32[]{:S(2)}, u32[]{:S(2)}) %collective-permute-start.12) | collective-permute-done | bytes 196640 | tf_op jit(solution)/shard_map/ppermute | solution.py:88
  202.7 5.1 %collective-permute-done.2 = f32[200,256]{1,0:T(8,128)S(1)} collective-permute-done((f32[200,256]{1,0:T(8,128)}, f32[200,256]{1,0:T(8,128)S(1)}, u32[]{:S(2)}, u32[]{:S(2)}) %collective-permute-start.2) | collective-permute-done | bytes 204832 | tf_op jit(solution)/shard_map/ppermute | solution.py:88
  (186 shorter events, 64.8 us)
Async XLA Ops:
  7.2 69.3 %copy-start = (bf16[256,3200]{1,0:T(8,128)(2,1)S(1)}, bf16[256,3200]{1,0:T(8,128)(2,1)}, u32[]{:S(2)}) copy-start(bf16[256,3200]{1,0:T(8,128)(2,1)} %param.19) | copy-start | bytes 4915204
  7.2 193.3 %reduce-scatter.2.cloned.1.call-start = ((), (), s32[]{:S(2)}) async-start(), calls=%async_computation.1 | async-start | bytes 3481600 | tf_op jit(solution)/shard_map/reduce_scatter | solution.py:222
  7.2 7.4 %collective-permute-start = (f32[1,6,3,100]{3,2,1,0:T(4,128)}, f32[1,6,3,100]{3,2,1,0:T(4,128)S(1)}, u32[]{:S(2)}, u32[]{:S(2)}) collective-permute-start(f32[1,6,3,100]{3,2,1,0:T(4,128)} %bitcast.239), channel_id=1, source_target_pairs={{0,1},{1,0},{2,3},{3,2},{4,5},{5,4},{6,7},{7,6},{8,9},{9,8},{10,11... | collective-permute-start | bytes 21608 | tf_op jit(solution)/shard_map/ppermute | solution.py:88
  25.4 27.6 %copy-start.20 = (f32[2,32,256]{2,1,0:T(8,128)S(1)}, f32[2,32,256]{2,1,0:T(8,128)}, u32[]{:S(2)}) copy-start(f32[2,32,256]{2,1,0:T(8,128)} %param.17) | copy-start | bytes 196612
  25.4 28.3 %copy-start.3 = (f32[6,200,256]{2,1,0:T(8,128)S(1)}, f32[6,200,256]{2,1,0:T(8,128)}, u32[]{:S(2)}) copy-start(f32[6,200,256]{2,1,0:T(8,128)} %copy-done.2) | copy-start | bytes 3686404
  25.4 28.3 %copy-start.11 = (f32[2,256,256]{2,1,0:T(8,128)S(1)}, f32[2,256,256]{2,1,0:T(8,128)}, u32[]{:S(2)}) copy-start(f32[2,256,256]{2,1,0:T(8,128)} %param.16) | copy-start | bytes 1572868
  55.3 34.9 %copy-start.5 = (f32[6,100,256]{2,1,0:T(8,128)}, f32[6,100,256]{2,1,0:T(8,128)S(1)}, u32[]{:S(2)}) copy-start(f32[6,100,256]{2,1,0:T(8,128)S(1)} %get-tuple-element.93) | copy-start | bytes 1843204
  56.0 5.8 %collective-permute-start.1 = (f32[1,6,100,32]{2,3,1,0:T(8,128)S(1)}, f32[1,6,100,32]{2,3,1,0:T(8,128)S(1)}, u32[]{:S(2)}, u32[]{:S(2)}) collective-permute-start(f32[1,6,100,32]{2,3,1,0:T(8,128)S(1)} %convolution_bitcast_fusion.2), channel_id=1, source_target_pairs={{0,1},{1,0},{2,3},{3,2},{4,5},{5,4},{6,7},{7,6},{8,9},{9,8},{10,11... | collective-permute-start | bytes 230408 | tf_op jit(solution)/shard_map/ppermute | solution.py:88
  64.3 8.8 %copy-start.12 = (f32[2,256,256]{2,1,0:T(8,128)S(1)}, f32[2,256,256]{2,1,0:T(8,128)}, u32[]{:S(2)}) copy-start(f32[2,256,256]{2,1,0:T(8,128)} %param.16) | copy-start | bytes 1572868
  112.4 4.7 %collective-permute-start.3 = (f32[1,6,100,32]{2,3,1,0:T(8,128)S(1)}, f32[1,6,100,32]{2,3,1,0:T(8,128)S(1)}, u32[]{:S(2)}, u32[]{:S(2)}) collective-permute-start(f32[1,6,100,32]{2,3,1,0:T(8,128)S(1)} %bitcast.237), channel_id=1, source_target_pairs={{0,1},{1,0},{2,3},{3,2},{4,5},{5,4},{6,7},{7,6},{8,9},{9,8},{10,11... | collective-permute-start | bytes 230408 | tf_op jit(solution)/shard_map/ppermute | solution.py:88
  142.5 6.7 %copy-start.6 = (f32[6,100,256]{2,1,0:T(8,128)S(1)}, f32[6,100,256]{2,1,0:T(8,128)}, u32[]{:S(2)}) copy-start(f32[6,100,256]{2,1,0:T(8,128)} %copy-done.5) | copy-start | bytes 1843204
  142.5 8.3 %collective-permute-start.4 = (f32[1,6,100,32]{2,3,1,0:T(8,128)}, f32[1,6,100,32]{2,3,1,0:T(8,128)}, u32[]{:S(2)}, u32[]{:S(2)}) collective-permute-start(f32[1,6,100,32]{2,3,1,0:T(8,128)} %bitcast.35), channel_id=1, source_target_pairs={{0,1},{1,0},{2,3},{3,2},{4,5},{5,4},{6,7},{7,6},{8,9},{9,8},{10,11... | collective-permute-start | bytes 230408 | tf_op jit(solution)/shard_map/ppermute | solution.py:88
  144.5 6.2 %copy-start.25 = (f32[1,32,256]{2,1,0:T(8,128)S(1)}, f32[1,32,256]{2,1,0:T(8,128)}, u32[]{:S(2)}) copy-start(f32[1,32,256]{2,1,0:T(8,128)} %convolution_bitcast_fusion.4) | copy-start | bytes 98308
  155.8 1.8 collective-permute-start.5
  157.6 7.0 %collective-permute-start.6 = (f32[4,48,256]{2,1,0:T(8,128)S(1)}, f32[4,48,256]{2,1,0:T(8,128)S(1)}, u32[]{:S(2)}, u32[]{:S(2)}) collective-permute-start(f32[4,48,256]{2,1,0:T(8,128)S(1)} %dynamic-slice_bitcast_fusion.1), channel_id=1, source_target_pairs={{0,4},{2,6},{4,0},{6,2},{8,12},{10,14},{12,8},{14,10},{16,20},{18,... | collective-permute-start | bytes 589832 | tf_op jit(solution)/shard_map/ppermute | solution.py:88
  164.7 4.7 %collective-permute-start.7 = (f32[2,48,256]{2,1,0:T(8,128)S(1)}, f32[2,48,256]{2,1,0:T(8,128)S(1)}, u32[]{:S(2)}, u32[]{:S(2)}) collective-permute-start(f32[2,48,256]{2,1,0:T(8,128)S(1)} %dynamic-slice_bitcast_fusion.2), channel_id=1, source_target_pairs={{0,8},{2,10},{4,12},{6,14},{8,0},{10,2},{12,4},{14,6},{16,24},{18,... | collective-permute-start | bytes 294920 | tf_op jit(solution)/shard_map/ppermute | solution.py:88
  169.4 7.1 %collective-permute-start.8 = (f32[1,48,256]{2,1,0:T(8,128)S(1)}, f32[1,48,256]{2,1,0:T(8,128)S(1)}, u32[]{:S(2)}, u32[]{:S(2)}) collective-permute-start(f32[1,48,256]{2,1,0:T(8,128)S(1)} %constant_dynamic-slice_fusion), channel_id=1, source_target_pairs={{0,16},{2,18},{4,20},{6,22},{8,24},{10,26},{12,28},{14,30},{16,0},... | collective-permute-start | bytes 147464 | tf_op jit(solution)/shard_map/ppermute | solution.py:88
  176.5 4.2 %collective-permute-start.9 = (f32[1,48,256]{2,1,0:T(8,128)S(1)}, f32[1,48,256]{2,1,0:T(8,128)S(1)}, u32[]{:S(2)}, u32[]{:S(2)}) collective-permute-start(f32[1,48,256]{2,1,0:T(8,128)S(1)} %dynamic-slice_add_fusion.1), channel_id=1, source_target_pairs={{0,1},{1,0},{2,3},{3,2},{4,5},{5,4},{6,7},{7,6},{8,9},{9,8},{10,11... | collective-permute-start | bytes 147464 | tf_op jit(solution)/shard_map/ppermute | solution.py:88
  180.7 5.2 %collective-permute-start.10 = (f32[1,48,256]{2,1,0:T(8,128)S(1)}, f32[1,48,256]{2,1,0:T(8,128)S(1)}, u32[]{:S(2)}, u32[]{:S(2)}) collective-permute-start(f32[1,48,256]{2,1,0:T(8,128)S(1)} %add.262), channel_id=1, source_target_pairs={{0,16},{2,18},{4,20},{6,22},{8,24},{10,26},{12,28},{14,30},{16,0},... | collective-permute-start | bytes 147464 | tf_op jit(solution)/shard_map/ppermute | solution.py:88
  185.9 4.7 %collective-permute-start.11 = (f32[2,48,256]{2,1,0:T(8,128)S(1)}, f32[2,48,256]{2,1,0:T(8,128)S(1)}, u32[]{:S(2)}, u32[]{:S(2)}) collective-permute-start(f32[2,48,256]{2,1,0:T(8,128)S(1)} %maximum_bitcast_fusion.1), channel_id=1, source_target_pairs={{0,8},{2,10},{4,12},{6,14},{8,0},{10,2},{12,4},{14,6},{16,24},{18,... | collective-permute-start | bytes 294920 | tf_op jit(solution)/shard_map/ppermute | solution.py:88
  190.6 5.7 %collective-permute-start.12 = (f32[4,48,256]{2,1,0:T(8,128)S(1)}, f32[4,48,256]{2,1,0:T(8,128)S(1)}, u32[]{:S(2)}, u32[]{:S(2)}) collective-permute-start(f32[4,48,256]{2,1,0:T(8,128)S(1)} %bitcast.232), channel_id=1, source_target_pairs={{0,4},{2,6},{4,0},{6,2},{8,12},{10,14},{12,8},{14,10},{16,20},{18,... | collective-permute-start | bytes 589832 | tf_op jit(solution)/shard_map/ppermute | solution.py:88
  196.4 1.8 collective-permute-start.13
  198.3 11.1 %copy-start.1 = (bf16[256,3200]{1,0:T(8,128)(2,1)S(1)}, bf16[256,3200]{1,0:T(8,128)(2,1)}, u32[]{:S(2)}) copy-start(bf16[256,3200]{1,0:T(8,128)(2,1)} %param.19) | copy-start | bytes 4915204
  200.5 7.3 %collective-permute-start.2 = (f32[200,256]{1,0:T(8,128)}, f32[200,256]{1,0:T(8,128)S(1)}, u32[]{:S(2)}, u32[]{:S(2)}) collective-permute-start(f32[200,256]{1,0:T(8,128)} %reduce-scatter.2.cloned.1.call-done), channel_id=1, source_target_pairs={{0,1},{1,0},{2,3},{3,2},{4,5},{5,4},{6,7},{7,6},{8,9},{9,8},{10,11... | collective-permute-start | bytes 614408 | tf_op jit(solution)/shard_map/ppermute | solution.py:88
  (25 other events, 81.2 us)
Sparse Core Ops, SparseCore 0:
  116.0 67.7 reduce-scatter.1

commit v3 on v2

--- a/solution.py
+++ b/solution.py
@@ -219,7 +219,7 @@
     d_states = lax.dot_general(d_orb, w_head, (((1,), (1,)), ((), ())), preferred_element_type=F32)
     d_states = d_states.reshape(states2.shape)
     head = lax.dot_general(d_orb, last, (((0,), (0,)), ((), ())), preferred_element_type=F32)
-    head_part = lax.psum_scatter(head, "walk", scatter_dimension=0, tiled=True)
+    head_part = sum_scatter(head.reshape(walk_size, -1, head.shape[1]), "walk")[0]
 
     def back(d_out, h, act, message, t, rows_l, layer):
         d_pre = d_out * (1.0 - act * act)

time: 217 us -> 230 us (1.060)
  local copies, waits for them, and re-layouts: 32.2 us -> 49.9 us
  between operations: 14.9 us -> 1.51 us
  starting transfers between devices: 17.2 us -> 23.8 us
  matrix products: 38.6 us -> 34.5 us
  waiting for transfers between devices: 38.4 us -> 42 us
  other arithmetic: 8.01 us -> 11.4 us
    dot_general x0 -> x1, local copies, waits for them, and re-layouts: none -> 6.8 us  [on_device(): lax.dot_general(d_orb, last, (((0,), (0,)), ((), ())), preferred_element_...]
    ppermute x14 -> x18, starting transfers between devices: 17.1 us -> 23.8 us  [swap(): return lax.ppermute(x, axis, [(i, i ^ bit) for i in range(size)])]
    another operation x6, local copies, waits for them, and re-layouts: 1.23 us -> 5.05 us
    ppermute x14 -> x18, waiting for transfers between devices: 38.3 us -> 42 us  [swap(): return lax.ppermute(x, axis, [(i, i ^ bit) for i in range(size)])]
    unnamed x70 -> x68, local copies, waits for them, and re-layouts: 4 us -> 5.46 us
  transfers between devices with their start and end apart: 15 -> 18, of which waited for: 11 -> 10; matrix products, arithmetic and copies ran while one was open for 17% -> 16% of each run, Pallas kernels for 8% -> 0%
where the time goes in v3:
time: 230 us; the launch traced here: 229 us
  Pallas kernels  66.1 us (29%)
  local copies, waits for them, and re-layouts  49.9 us (22%)
  waiting for transfers between devices  42 us (18%)
  matrix products  34.5 us (15%)
  starting transfers between devices  23.8 us (10%)
  other arithmetic  11.4 us (5%)
    ppermute x18, waiting for transfers between devices, swap(): return lax.ppermute(x, axis, [(i, i ^ bit) for i in range(size)])  42 us
    pallas_call x2, Pallas kernels, back(): pl.pallas_call(functools.partial(back_kernel, groups, rows), grid=(own,),...  32 us
    pallas_call x1, Pallas kernels, on_device(): pl.pallas_call(functools.partial(pair_kernel, groups, rows), grid=(own,),...  26 us
    ppermute x18, starting transfers between devices, swap(): return lax.ppermute(x, axis, [(i, i ^ bit) for i in range(size)])  23.8 us
    pallas_call x1, Pallas kernels, on_device(): pl.pallas_call(functools.partial(message_kernel, groups, rows), grid=(own...  8.12 us
    dot_general x1, local copies, waits for them, and re-layouts, on_device(): lax.dot_general(d_orb, last, (((0,), (0,)), ((), ())), preferred_element_...  6.8 us
    convert_element_type x1, local copies, waits for them, and re-layouts, on_device(): flat_targets = targets.reshape(-1, targets.shape[2]).astype(F32)  5.6 us
    unnamed x68, local copies, waits for them, and re-layouts  5.46 us
  transfers between devices with their start and end apart: 18, of which 10 were waited for; matrix products, arithmetic and copies ran while one was open for 16% of the time, Pallas kernels for 0%

profile of v3, /device:TPU:0, one launch (start us, length us, event | category | flops | bytes accessed | tf_op | source)
XLA Modules:
  0.0 229.2 jit_solution(6416482828278230019)
XLA Ops:
  0.6 3.0 %collective-permute-start = (f32[1,6,3,100]{3,2,1,0:T(4,128)}, f32[1,6,3,100]{3,2,1,0:T(4,128)S(1)}, u32[]{:S(2)}, u32[]{:S(2)}) collective-permute-start(f32[1,6,3,100]{3,2,1,0:T(4,128)} %bitcast.266), channel_id=1, source_target_pairs={{0,1},{1,0},{2,3},{3,2},{4,5},{5,4},{6,7},{7,6},{8,9},{9,8},{10,11... | collective-permute-start | bytes 21608 | tf_op jit(solution)/shard_map/ppermute | solution.py:88
  16.8 2.7 %reshape.177 = f32[6,25,3,256]{3,1,2,0:T(8,128)} reshape(f32[6,25,3,8,32]{4,3,1,2,0:T(8,128)} %broadcast_in_dim.13) | data formatting | bytes 921600 | tf_op jit(solution)/shard_map/reshape | solution.py:157
  21.0 26.0 %shard_map.153 = (f32[6,25,104,256]{3,2,1,0:T(8,128)}, f32[6,25,104,256]{3,2,1,0:T(8,128)}, f32[6,25,104,256]{3,2,1,0:T(8,128)}, f32[6,104,32]{2,1,0:T(8,128)S(1)}) custom-call(f32[6,104,3]{2,1,0:T(8,128)S(1)} %pad.15.xi_ref, f32[6,25,3,256]{3,2,1,0:T(4,128)S(1)} %copy.172.xj_ref, f32[4,256]{1,0:T(4,128)S(1)} %tile.9.v_ref, ...), custom_call_target="tpu_custom_call" | custom-call | tf_op jit(solution)/shard_map/pallas_call | solution.py:177
  50.2 5.6 %reshape.199 = f32[600,3200]{1,0:T(8,128)} reshape(bf16[6,100,3200]{2,1,0:T(8,128)(2,1)} %param.11) | data formatting | bytes 11520000 | tf_op jit(solution)/shard_map/convert_element_type | solution.py:217
  58.4 8.1 %shard_map.154 = f32[6,104,32]{2,1,0:T(8,128)S(1)} custom-call(f32[6,25,104,256]{3,2,1,0:T(8,128)} %get-tuple-element.16.t_ref, f32[6,25,1,256]{3,2,1,0:T(1,128)S(1)} %reshape.217.proj_ref, f32[256,32]{1,0:T(8,128)S(1)} %bitcast.238), custom_call_target="tpu_custom_call" | custom-call | tf_op jit(solution)/shard_map/pallas_call | solution.py:203
  70.5 4.5 %multiply_convert_fusion = bf16[600,3200]{1,0:T(8,128)(2,1)S(1)} fusion(f32[600,3200]{1,0:T(8,128)} %reshape.199, bf16[600,256]{1,0:T(8,128)(2,1)} %convert_element_type.31, bf16[256,3200]{1,0:T(8,128)(2,1)S(1)} %copy-done), kind=kOutput, calls=%fused_computation | convolution fusion | flops 988800000 | bytes 13465600 | tf_op jit(solution)/shard_map/dot_general | solution.py:216
  76.9 2.1 fusion.61
  86.2 16.0 %shard_map.155 = (f32[6,25,1,256]{3,2,1,0:T(1,128)S(1)}, f32[256,256]{1,0:T(8,128)S(1)}) custom-call(f32[6,25,104,256]{3,2,1,0:T(8,128)} %get-tuple-element.17.pairs_ref, f32[6,25,104,256]{3,2,1,0:T(8,128)} %get-tuple-element.16.t_ref, f32[6,25,1,256]{3,2,1,0:T(1,128)S(1)} %reshape.217.proj_ref, f32[6,104,32]{2,1,0:T(8,128)S(1)} %pad.16.dm_ref), custom_call_target="tpu_custom_call" | custom-call | tf_op jit(solution)/shard_map/pallas_call | solution.py:231
  110.7 6.8 %copy.178 = bf16[3200,600]{1,0:T(8,128)(2,1)} copy(bf16[3200,600]{0,1:T(8,128)(2,1)} %bitcast.240) | data formatting | bytes 7680000 | tf_op jit(solution)/shard_map/dot_general | solution.py:221
  118.2 2.5 %fusion.58 = (f32[256]{0:T(256)}, f32[6,100,256]{2,1,0:T(8,128)S(1)}, f32[6,100,256]{2,1,0:T(8,128)S(1)}) fusion(f32[6,100,256]{2,1,0:T(8,128)S(1)} %copy-done.8, f32[6,100,256]{2,1,0:T(8,128)} %convolution_add_fusion.1, f32[2,256,32]{1,2,0:T(8,128)S(1)} %copy-done.20, f32[1,6,100,32]{2,3,1,0:T(8,128)} %copy-done.18, f32[6,1,100,32]{2,3,1,0:T(8,128)S(1)} %copy.182), kind=kOutput, calls=%fused_computation.137 | convolution fusion | flops 59769344 | bytes 2691072 | tf_op jit(solution)/shard_map/wjp,hp->wjh/dot_general | solution.py:251
  125.4 16.0 %shard_map.156 = (f32[6,25,1,256]{3,2,1,0:T(1,128)S(1)}, f32[256,256]{1,0:T(8,128)S(1)}) custom-call(f32[6,25,104,256]{3,2,1,0:T(8,128)} %get-tuple-element.17.pairs_ref, f32[6,25,104,256]{3,2,1,0:T(8,128)} %get-tuple-element.19.t_ref, f32[6,25,1,256]{3,2,1,0:T(1,128)S(1)} %reshape.216.proj_ref, f32[6,104,32]{2,1,0:T(8,128)S(1)} %pad.17.dm_ref), custom_call_target="tpu_custom_call" | custom-call | tf_op jit(solution)/shard_map/pallas_call | solution.py:231
  154.0 3.7 %fusion.8 = f32[8,2,200,256]{3,2,1,0:T(8,128)S(1)} fusion(bf16[8,2,200,600]{3,2,1,0:T(8,128)(2,1)} %bitcast.239, bf16[600,256,1,1]{1,0,2,3:T(8,128)(2,1)S(1)} %copy-done.14), kind=kOutput, calls=%fused_computation.46 | convolution fusion | flops 983040000 | bytes 7424000 | tf_op jit(solution)/shard_map/dot_general | solution.py:221
  162.1 5.3 %collective-permute-done.10 = f32[4,48,256]{2,1,0:T(8,128)S(1)} collective-permute-done((f32[4,48,256]{2,1,0:T(8,128)S(1)}, f32[4,48,256]{2,1,0:T(8,128)S(1)}, u32[]{:S(2)}, u32[]{:S(2)}) %collective-permute-start.10) | collective-permute-done | bytes 196640 | tf_op jit(solution)/shard_map/ppermute | solution.py:88
  169.1 3.0 %collective-permute-done.11 = f32[2,48,256]{2,1,0:T(8,128)S(1)} collective-permute-done((f32[2,48,256]{2,1,0:T(8,128)S(1)}, f32[2,48,256]{2,1,0:T(8,128)S(1)}, u32[]{:S(2)}, u32[]{:S(2)}) %collective-permute-start.11) | collective-permute-done | bytes 98336 | tf_op jit(solution)/shard_map/ppermute | solution.py:88
  172.2 2.7 %collective-permute-start.12 = (f32[1,48,256]{2,1,0:T(8,128)S(1)}, f32[1,48,256]{2,1,0:T(8,128)S(1)}, u32[]{:S(2)}, u32[]{:S(2)}) collective-permute-start(f32[1,48,256]{2,1,0:T(8,128)S(1)} %constant_dynamic-slice_fusion), channel_id=1, source_target_pairs={{0,16},{2,18},{4,20},{6,22},{8,24},{10,26},{12,28},{14,30},{16,0},... | collective-permute-start | bytes 147464 | tf_op jit(solution)/shard_map/ppermute | solution.py:88
  174.9 2.4 %collective-permute-done.12 = f32[1,48,256]{2,1,0:T(8,128)S(1)} collective-permute-done((f32[1,48,256]{2,1,0:T(8,128)S(1)}, f32[1,48,256]{2,1,0:T(8,128)S(1)}, u32[]{:S(2)}, u32[]{:S(2)}) %collective-permute-start.12) | collective-permute-done | bytes 49184 | tf_op jit(solution)/shard_map/ppermute | solution.py:88
  178.8 2.6 %collective-permute-done.13 = f32[1,48,256]{2,1,0:T(8,128)S(1)} collective-permute-done((f32[1,48,256]{2,1,0:T(8,128)S(1)}, f32[1,48,256]{2,1,0:T(8,128)S(1)}, u32[]{:S(2)}, u32[]{:S(2)}) %collective-permute-start.13) | collective-permute-done | bytes 49184 | tf_op jit(solution)/shard_map/ppermute | solution.py:88
  181.4 2.7 %collective-permute-start.14 = (f32[1,48,256]{2,1,0:T(8,128)S(1)}, f32[1,48,256]{2,1,0:T(8,128)S(1)}, u32[]{:S(2)}, u32[]{:S(2)}) collective-permute-start(f32[1,48,256]{2,1,0:T(8,128)S(1)} %add.292), channel_id=1, source_target_pairs={{0,16},{2,18},{4,20},{6,22},{8,24},{10,26},{12,28},{14,30},{16,0},... | collective-permute-start | bytes 147464 | tf_op jit(solution)/shard_map/ppermute | solution.py:88
  189.5 2.8 %collective-permute-done.15 = f32[2,48,256]{2,1,0:T(8,128)} collective-permute-done((f32[2,48,256]{2,1,0:T(8,128)S(1)}, f32[2,48,256]{2,1,0:T(8,128)}, u32[]{:S(2)}, u32[]{:S(2)}) %collective-permute-start.15) | collective-permute-done | bytes 98336 | tf_op jit(solution)/shard_map/ppermute | solution.py:88
  193.8 10.0 %collective-permute-done.3 = f32[4,200,256]{2,1,0:T(8,128)S(1)} collective-permute-done((f32[4,200,256]{2,1,0:T(8,128)S(1)}, f32[4,200,256]{2,1,0:T(8,128)S(1)}, u32[]{:S(2)}, u32[]{:S(2)}) %collective-permute-start.3) | collective-permute-done | bytes 819232 | tf_op jit(solution)/shard_map/ppermute | solution.py:88
  204.0 2.1 collective-permute-start.4
  207.1 6.5 %collective-permute-done.4 = f32[2,200,256]{2,1,0:T(8,128)S(1)} collective-permute-done((f32[2,200,256]{2,1,0:T(8,128)S(1)}, f32[2,200,256]{2,1,0:T(8,128)S(1)}, u32[]{:S(2)}, u32[]{:S(2)}) %collective-permute-start.4) | collective-permute-done | bytes 409632 | tf_op jit(solution)/shard_map/ppermute | solution.py:88
  216.8 5.9 %collective-permute-done.5 = f32[1,200,256]{2,1,0:T(8,128)S(1)} collective-permute-done((f32[1,200,256]{2,1,0:T(8,128)S(1)}, f32[1,200,256]{2,1,0:T(8,128)S(1)}, u32[]{:S(2)}, u32[]{:S(2)}) %collective-permute-start.5) | collective-permute-done | bytes 204832 | tf_op jit(solution)/shard_map/ppermute | solution.py:88
  225.7 2.8 %collective-permute-done.6 = f32[200,256]{1,0:T(8,128)S(1)} collective-permute-done((f32[200,256]{1,0:T(8,128)S(1)}, f32[200,256]{1,0:T(8,128)S(1)}, u32[]{:S(2)}, u32[]{:S(2)}) %collective-permute-start.6) | collective-permute-done | bytes 204832 | tf_op jit(solution)/shard_map/ppermute | solution.py:88
  (199 shorter events, 81.7 us)
Async XLA Ops:
  0.6 69.9 %copy-start = (bf16[256,3200]{1,0:T(8,128)(2,1)S(1)}, bf16[256,3200]{1,0:T(8,128)(2,1)}, u32[]{:S(2)}) copy-start(bf16[256,3200]{1,0:T(8,128)(2,1)} %param.19) | copy-start | bytes 4915204
  0.6 8.2 %collective-permute-start = (f32[1,6,3,100]{3,2,1,0:T(4,128)}, f32[1,6,3,100]{3,2,1,0:T(4,128)S(1)}, u32[]{:S(2)}, u32[]{:S(2)}) collective-permute-start(f32[1,6,3,100]{3,2,1,0:T(4,128)} %bitcast.266), channel_id=1, source_target_pairs={{0,1},{1,0},{2,3},{3,2},{4,5},{5,4},{6,7},{7,6},{8,9},{9,8},{10,11... | collective-permute-start | bytes 21608 | tf_op jit(solution)/shard_map/ppermute | solution.py:88
  19.6 27.5 %copy-start.22 = (f32[2,32,256]{2,1,0:T(8,128)S(1)}, f32[2,32,256]{2,1,0:T(8,128)}, u32[]{:S(2)}) copy-start(f32[2,32,256]{2,1,0:T(8,128)} %param.17) | copy-start | bytes 196612
  21.0 26.7 %copy-start.3 = (f32[6,200,256]{2,1,0:T(8,128)S(1)}, f32[6,200,256]{2,1,0:T(8,128)}, u32[]{:S(2)}) copy-start(f32[6,200,256]{2,1,0:T(8,128)} %copy-done.2) | copy-start | bytes 3686404
  21.0 26.7 %copy-start.9 = (f32[2,256,256]{2,1,0:T(8,128)S(1)}, f32[2,256,256]{2,1,0:T(8,128)}, u32[]{:S(2)}) copy-start(f32[2,256,256]{2,1,0:T(8,128)} %param.16) | copy-start | bytes 1572868
  50.0 5.7 %collective-permute-start.1 = (f32[1,6,100,32]{2,3,1,0:T(8,128)S(1)}, f32[1,6,100,32]{2,3,1,0:T(8,128)S(1)}, u32[]{:S(2)}, u32[]{:S(2)}) collective-permute-start(f32[1,6,100,32]{2,3,1,0:T(8,128)S(1)} %convolution_bitcast_fusion.2), channel_id=1, source_target_pairs={{0,1},{1,0},{2,3},{3,2},{4,5},{5,4},{6,7},{7,6},{8,9},{9,8},{10,11... | collective-permute-start | bytes 230408 | tf_op jit(solution)/shard_map/ppermute | solution.py:88
  58.3 8.8 %copy-start.10 = (f32[2,256,256]{2,1,0:T(8,128)S(1)}, f32[2,256,256]{2,1,0:T(8,128)}, u32[]{:S(2)}) copy-start(f32[2,256,256]{2,1,0:T(8,128)} %param.16) | copy-start | bytes 1572868
  106.5 11.0 %collective-permute-start.7 = (f32[1,6,100,32]{2,3,1,0:T(8,128)S(1)}, f32[1,6,100,32]{2,3,1,0:T(8,128)S(1)}, u32[]{:S(2)}, u32[]{:S(2)}) collective-permute-start(f32[1,6,100,32]{2,3,1,0:T(8,128)S(1)} %bitcast.263), channel_id=1, source_target_pairs={{0,1},{1,0},{2,3},{3,2},{4,5},{5,4},{6,7},{7,6},{8,9},{9,8},{10,11... | collective-permute-start | bytes 230408 | tf_op jit(solution)/shard_map/ppermute | solution.py:88
  145.8 4.7 %collective-permute-start.8 = (f32[1,6,100,32]{2,3,1,0:T(8,128)S(1)}, f32[1,6,100,32]{2,3,1,0:T(8,128)S(1)}, u32[]{:S(2)}, u32[]{:S(2)}) collective-permute-start(f32[1,6,100,32]{2,3,1,0:T(8,128)S(1)} %bitcast.264), channel_id=1, source_target_pairs={{0,1},{1,0},{2,3},{3,2},{4,5},{5,4},{6,7},{7,6},{8,9},{9,8},{10,11... | collective-permute-start | bytes 230408 | tf_op jit(solution)/shard_map/ppermute | solution.py:88
  153.9 6.5 %collective-permute-start.9 = (f32[8,48,256]{2,1,0:T(8,128)S(1)}, f32[8,48,256]{2,1,0:T(8,128)S(1)}, u32[]{:S(2)}, u32[]{:S(2)}) collective-permute-start(f32[8,48,256]{2,1,0:T(8,128)S(1)} %dynamic-slice_bitcast_fusion.3), channel_id=1, source_target_pairs={{0,2},{2,0},{4,6},{6,4},{8,10},{10,8},{12,14},{14,12},{16,18},{18,... | collective-permute-start | bytes 1179656 | tf_op jit(solution)/shard_map/ppermute | solution.py:88
  159.9 24.2 %collective-permute-start.2 = (f32[8,200,256]{2,1,0:T(8,128)}, f32[8,200,256]{2,1,0:T(8,128)S(1)}, u32[]{:S(2)}, u32[]{:S(2)}) collective-permute-start(f32[8,200,256]{2,1,0:T(8,128)} %dynamic-slice_bitcast_fusion), channel_id=1, source_target_pairs={{0,2},{2,0},{4,6},{6,4},{8,10},{10,8},{12,14},{14,12},{16,18},{18,... | collective-permute-start | bytes 4915208 | tf_op jit(solution)/shard_map/ppermute | solution.py:88
  160.5 6.9 %collective-permute-start.10 = (f32[4,48,256]{2,1,0:T(8,128)S(1)}, f32[4,48,256]{2,1,0:T(8,128)S(1)}, u32[]{:S(2)}, u32[]{:S(2)}) collective-permute-start(f32[4,48,256]{2,1,0:T(8,128)S(1)} %dynamic-slice_bitcast_fusion.4), channel_id=1, source_target_pairs={{0,4},{2,6},{4,0},{6,2},{8,12},{10,14},{12,8},{14,10},{16,20},{18,... | collective-permute-start | bytes 589832 | tf_op jit(solution)/shard_map/ppermute | solution.py:88
  167.5 4.7 %collective-permute-start.11 = (f32[2,48,256]{2,1,0:T(8,128)S(1)}, f32[2,48,256]{2,1,0:T(8,128)S(1)}, u32[]{:S(2)}, u32[]{:S(2)}) collective-permute-start(f32[2,48,256]{2,1,0:T(8,128)S(1)} %dynamic-slice_bitcast_fusion.5), channel_id=1, source_target_pairs={{0,8},{2,10},{4,12},{6,14},{8,0},{10,2},{12,4},{14,6},{16,24},{18,... | collective-permute-start | bytes 294920 | tf_op jit(solution)/shard_map/ppermute | solution.py:88
  172.2 5.1 %collective-permute-start.12 = (f32[1,48,256]{2,1,0:T(8,128)S(1)}, f32[1,48,256]{2,1,0:T(8,128)S(1)}, u32[]{:S(2)}, u32[]{:S(2)}) collective-permute-start(f32[1,48,256]{2,1,0:T(8,128)S(1)} %constant_dynamic-slice_fusion), channel_id=1, source_target_pairs={{0,16},{2,18},{4,20},{6,22},{8,24},{10,26},{12,28},{14,30},{16,0},... | collective-permute-start | bytes 147464 | tf_op jit(solution)/shard_map/ppermute | solution.py:88
  177.3 4.2 %collective-permute-start.13 = (f32[1,48,256]{2,1,0:T(8,128)S(1)}, f32[1,48,256]{2,1,0:T(8,128)S(1)}, u32[]{:S(2)}, u32[]{:S(2)}) collective-permute-start(f32[1,48,256]{2,1,0:T(8,128)S(1)} %dynamic-slice_add_fusion.1), channel_id=1, source_target_pairs={{0,1},{1,0},{2,3},{3,2},{4,5},{5,4},{6,7},{7,6},{8,9},{9,8},{10,11... | collective-permute-start | bytes 147464 | tf_op jit(solution)/shard_map/ppermute | solution.py:88
  181.4 6.0 %collective-permute-start.14 = (f32[1,48,256]{2,1,0:T(8,128)S(1)}, f32[1,48,256]{2,1,0:T(8,128)S(1)}, u32[]{:S(2)}, u32[]{:S(2)}) collective-permute-start(f32[1,48,256]{2,1,0:T(8,128)S(1)} %add.292), channel_id=1, source_target_pairs={{0,16},{2,18},{4,20},{6,22},{8,24},{10,26},{12,28},{14,30},{16,0},... | collective-permute-start | bytes 147464 | tf_op jit(solution)/shard_map/ppermute | solution.py:88
  185.9 17.9 %collective-permute-start.3 = (f32[4,200,256]{2,1,0:T(8,128)S(1)}, f32[4,200,256]{2,1,0:T(8,128)S(1)}, u32[]{:S(2)}, u32[]{:S(2)}) collective-permute-start(f32[4,200,256]{2,1,0:T(8,128)S(1)} %dynamic-slice_bitcast_fusion.1), channel_id=1, source_target_pairs={{0,4},{2,6},{4,0},{6,2},{8,12},{10,14},{12,8},{14,10},{16,20},{18,... | collective-permute-start | bytes 2457608 | tf_op jit(solution)/shard_map/ppermute | solution.py:88
  187.4 4.8 %collective-permute-start.15 = (f32[2,48,256]{2,1,0:T(8,128)S(1)}, f32[2,48,256]{2,1,0:T(8,128)}, u32[]{:S(2)}, u32[]{:S(2)}) collective-permute-start(f32[2,48,256]{2,1,0:T(8,128)S(1)} %maximum_bitcast_fusion.1), channel_id=1, source_target_pairs={{0,8},{2,10},{4,12},{6,14},{8,0},{10,2},{12,4},{14,6},{16,24},{18,... | collective-permute-start | bytes 294920 | tf_op jit(solution)/shard_map/ppermute | solution.py:88
  193.2 12.8 %collective-permute-start.16 = (f32[4,48,256]{2,1,0:T(8,128)S(1)}, f32[4,48,256]{2,1,0:T(8,128)}, u32[]{:S(2)}, u32[]{:S(2)}) collective-permute-start(f32[4,48,256]{2,1,0:T(8,128)S(1)} %bitcast.258), channel_id=1, source_target_pairs={{0,4},{2,6},{4,0},{6,2},{8,12},{10,14},{12,8},{14,10},{16,20},{18,... | collective-permute-start | bytes 589832 | tf_op jit(solution)/shard_map/ppermute | solution.py:88
  204.0 9.7 %collective-permute-start.4 = (f32[2,200,256]{2,1,0:T(8,128)S(1)}, f32[2,200,256]{2,1,0:T(8,128)S(1)}, u32[]{:S(2)}, u32[]{:S(2)}) collective-permute-start(f32[2,200,256]{2,1,0:T(8,128)S(1)} %dynamic-slice_bitcast_fusion.2), channel_id=1, source_target_pairs={{0,8},{2,10},{4,12},{6,14},{8,0},{10,2},{12,4},{14,6},{16,24},{18,... | collective-permute-start | bytes 1228808 | tf_op jit(solution)/shard_map/ppermute | solution.py:88
  207.0 6.8 %collective-permute-start.17 = (f32[8,48,256]{2,1,0:T(8,128)S(1)}, f32[8,48,256]{2,1,0:T(8,128)S(1)}, u32[]{:S(2)}, u32[]{:S(2)}) collective-permute-start(f32[8,48,256]{2,1,0:T(8,128)S(1)} %bitcast.253), channel_id=1, source_target_pairs={{0,2},{2,0},{4,6},{6,4},{8,10},{10,8},{12,14},{14,12},{16,18},{18,... | collective-permute-start | bytes 1179656 | tf_op jit(solution)/shard_map/ppermute | solution.py:88
  213.8 8.9 %collective-permute-start.5 = (f32[1,200,256]{2,1,0:T(8,128)S(1)}, f32[1,200,256]{2,1,0:T(8,128)S(1)}, u32[]{:S(2)}, u32[]{:S(2)}) collective-permute-start(f32[1,200,256]{2,1,0:T(8,128)S(1)} %constant_dynamic-slice_fusion.5), channel_id=1, source_target_pairs={{0,16},{2,18},{4,20},{6,22},{8,24},{10,26},{12,28},{14,30},{16,0},... | collective-permute-start | bytes 614408 | tf_op jit(solution)/shard_map/ppermute | solution.py:88
  214.0 15.2 %copy-start.1 = (bf16[256,3200]{1,0:T(8,128)(2,1)S(1)}, bf16[256,3200]{1,0:T(8,128)(2,1)}, u32[]{:S(2)}) copy-start(bf16[256,3200]{1,0:T(8,128)(2,1)} %param.19) | copy-start | bytes 4915204
  222.7 5.8 %collective-permute-start.6 = (f32[200,256]{1,0:T(8,128)S(1)}, f32[200,256]{1,0:T(8,128)S(1)}, u32[]{:S(2)}, u32[]{:S(2)}) collective-permute-start(f32[200,256]{1,0:T(8,128)S(1)} %add_bitcast_fusion), channel_id=1, source_target_pairs={{0,1},{1,0},{2,3},{3,2},{4,5},{5,4},{6,7},{7,6},{8,9},{9,8},{10,11... | collective-permute-start | bytes 614408 | tf_op jit(solution)/shard_map/ppermute | solution.py:88
  (27 other events, 88.4 us)
